TPU v7x, 256 devices: a whole 4x4x8 slice. The times are simulated.
256 devices in a mesh: dp: 64 (over y_lo, x, z), tok: 4 (over y_hi, core).
Axes of the slice: x: 4, y: 4 (y_hi: 2, y_lo: 2; y = y_hi * 2 + y_lo), z: 8, core: 2. Of those that a mesh axis runs over, the one named last changes fastest.
Arguments:
- queries: bfloat16 [4096, 32, 128], P('dp'), may hold values from -6 to 6
- documents: bfloat16 [8192, 180, 128], P('dp', 'tok'), may hold values from -6 to 6
- lengths: int32 [8192], replicated, may hold values from 1 to 180
Outputs:
- scores: float32 [4096, 2, 128], P('dp')
All inputs are finite; a program needn't handle non-finite values.
Results may differ from a plain program's by a relative error of at most 0.00034.
Values may be sent and summed in bfloat16 or wider, within the bound.
No kernel may reach another device: no remote copies, remote signals or barrier semaphores. Data moves between devices by JAX's collectives and lax.ppermute only.
A program may use at most 64 MiB of HBM per device.

v0:
```python
import jax
import jax.numpy as jnp
from jax import lax
from jax.sharding import PartitionSpec as P

STEPS = 2


negative_fill = -1e30


def shifted(block, axis, distance):
    devices = range(lax.axis_size(axis))
    route = [((i - distance) % len(devices), i) for i in devices]
    return lax.ppermute(block, axis, route)


def normalize(values):
    wide = values.astype(jnp.float32)
    return (wide * lax.rsqrt(jnp.sum(wide * wide, axis=-1, keepdims=True) + 1e-06)).astype(
        jnp.bfloat16
    )


def slot_group(count):
    best_size = 1
    for trial in range(1, 9):
        if count % trial == 0:
            best_size = trial
    return best_size


def token_maxima(shard_q, token_major, limits_all, offset):
    qcount, query_len, embed_width = shard_q.shape
    doc_len, dcount, _ = token_major.shape
    group = slot_group(doc_len)
    flat_q = shard_q.reshape(qcount * query_len, embed_width)
    grouped = token_major.reshape(doc_len // group, group * dcount, embed_width)
    position = (offset + jnp.arange(doc_len, dtype=jnp.int32)).reshape(doc_len // group, group)

    def one_group(running, operands):
        doc_tile, slots = operands
        similar = lax.dot_general(
            flat_q, doc_tile, (((1,), (1,)), ((), ())), preferred_element_type=jnp.float32
        )
        similar = similar.reshape(qcount * query_len, group, dcount)
        usable = slots[:, None] < limits_all[None, :]
        similar = jnp.where(usable[None], similar, negative_fill)
        return (jnp.maximum(running, jnp.max(similar, axis=1)), None)

    start = jnp.full((qcount * query_len, dcount), negative_fill, jnp.float32)
    maxima, _ = lax.scan(one_group, start, (grouped, position))
    return maxima.reshape(qcount, query_len, dcount)


def combine(maxima):
    merged = lax.pmax(maxima, "tok")
    return jnp.sum(merged, axis=1)


def per_device(queries, documents, lengths):
    shard_q = normalize(queries)
    shard_d = jnp.transpose(normalize(documents), (1, 0, 2))
    loop_size = lax.axis_size("dp")
    cycle_index = lax.axis_index("dp")
    doc_dev = documents.shape[0]
    offset = lax.axis_index("tok") * documents.shape[1]
    results = []
    moving = shard_d
    for step_no in range(STEPS):
        moving = shifted(moving, "dp", 1)
        limits = lax.dynamic_slice_in_dim(
            lengths, (cycle_index - 1 - step_no + loop_size) % loop_size * doc_dev, doc_dev, 0
        )
        results.append(combine(token_maxima(shard_q, moving, limits, offset)))
    return jnp.stack(results, axis=1)


def solution(mesh):
    in_specs = (P("dp", None, None), P("dp", "tok", None), P())
    out_specs = P("dp", None, None)
    return jax.shard_map(
        per_device, mesh=mesh, in_specs=in_specs, out_specs=out_specs, check_vma=False
    )
```

profile of v0, /device:TPU:1, one launch (start us, length us, event | category | flops | bytes accessed | tf_op | source)
XLA Modules:
  0.0 188.0 jit_solution(16982997468788430056)
XLA Ops:
  6.5 2.3 %fusion.8 = f32[128,45]{0,1:T(8,128)S(1)} fusion(bf16[128,45,128]{2,0,1:T(8,128)(2,1)} %param.8), kind=kLoop, calls=%fused_computation.18 | loop fusion | flops 2206080 | bytes 1497600 | tf_op jit(solution)/shard_map/reduce_sum | solution.py:20
  8.8 2.9 %fusion.10 = bf16[45,128,128]{2,1,0:T(8,128)(2,1)} fusion(bf16[128,45,128]{2,0,1:T(8,128)(2,1)} %param.8, f32[128,45]{0,1:T(8,128)S(1)} %add_rsqrt_fusion.1), kind=kLoop, calls=%fused_computation.20 | loop fusion | flops 2211840 | bytes 2972160 | tf_op jit(solution)/shard_map/transpose | solution.py:63
  11.8 2.5 %collective-permute-start = (bf16[45,128,128]{2,1,0:T(8,128)(2,1)}, bf16[45,128,128]{2,1,0:T(8,128)(2,1)}, u32[]{:S(2)}, u32[]{:S(2)}) collective-permute-start(bf16[45,128,128]{2,1,0:T(8,128)(2,1)} %fusion.10), channel_id=1, source_target_pairs={{252,0},{0,4},{4,8},{8,12},{12,16},{16,20},{20,24},{24,28},{28,32}... | collective-permute-start | bytes 4423688 | tf_op jit(solution)/shard_map/ppermute | solution.py:15
  14.2 0.8 fusion.13
  15.1 0.3 fusion.11
  15.8 37.9 %collective-permute-done = bf16[45,128,128]{2,1,0:T(8,128)(2,1)} collective-permute-done((bf16[45,128,128]{2,1,0:T(8,128)(2,1)}, bf16[45,128,128]{2,1,0:T(8,128)(2,1)}, u32[]{:S(2)}, u32[]{:S(2)}) %collective-permute-start) | collective-permute-done | bytes 1474592 | tf_op jit(solution)/shard_map/ppermute | solution.py:15
  53.7 25.7 %while.22 = (s32[]{:T(128)}, f32[2048,128]{0,1:T(8,128)S(1)}, s32[9,5]{1,0:T(8,128)S(1)}, s32[128]{0:T(128)S(1)}, bf16[9,640,128]{2,1,0:T(8,128)(2,1)}, /*index=5*/bf16[2048,128]{1,0:T(8,128)(2,1)S(1)}, s32[]{:T(128)}, s32[]{:T(128)}) while((s32[]{:T(128)}, f32[2048,128]{0,1:T(8,128)S(1)}, s32[9,5]{1,0:T(8,128)S(1)}, ...), condition=%wide.region_4.5_spmd.clone, body=%wide.region_2.4_spmd.clone.sunk | while | flops 338428544 | bytes 15370155 | solution.py:52
  53.8 1.8 fusion.24
  55.6 0.6 select_reduce_fusion.4
  56.2 0.3 select_maximum_fusion.4
  56.7 1.8 fusion.24
  58.4 0.6 select_reduce_fusion.4
  59.1 0.3 select_maximum_fusion.4
  59.5 1.8 fusion.24
  61.3 0.6 select_reduce_fusion.4
  61.9 0.3 select_maximum_fusion.4
  62.4 1.8 fusion.24
  64.1 0.6 select_reduce_fusion.4
  64.8 0.3 select_maximum_fusion.4
  65.2 1.8 fusion.24
  67.0 0.6 select_reduce_fusion.4
  67.6 0.3 select_maximum_fusion.4
  68.1 1.8 fusion.24
  69.9 0.6 select_reduce_fusion.4
  70.5 0.3 select_maximum_fusion.4
  71.0 1.8 fusion.24
  72.7 0.6 select_reduce_fusion.4
  73.4 0.3 select_maximum_fusion.4
  73.8 1.8 fusion.24
  75.6 0.6 select_reduce_fusion.4
  76.2 0.3 select_maximum_fusion.4
  76.7 1.8 fusion.24
  78.4 0.6 select_reduce_fusion.4
  79.1 0.3 select_maximum_fusion.4
  79.4 1.3 copy.4
  80.7 10.1 %collective-permute-done.1 = bf16[45,128,128]{2,1,0:T(8,128)(2,1)} collective-permute-done((bf16[45,128,128]{2,1,0:T(8,128)(2,1)}, bf16[45,128,128]{2,1,0:T(8,128)(2,1)}, u32[]{:S(2)}, u32[]{:S(2)}) %collective-permute-start.1) | collective-permute-done | bytes 1474592 | tf_op jit(solution)/shard_map/ppermute | solution.py:15
  90.8 25.7 %while.23 = (s32[]{:T(128)}, f32[2048,128]{0,1:T(8,128)S(1)}, s32[9,5]{1,0:T(8,128)S(1)}, s32[128]{0:T(128)S(1)}, bf16[9,640,128]{2,1,0:T(8,128)(2,1)}, /*index=5*/bf16[2048,128]{1,0:T(8,128)(2,1)S(1)}, s32[]{:T(128)}, s32[]{:T(128)}) while((s32[]{:T(128)}, f32[2048,128]{0,1:T(8,128)S(1)}, s32[9,5]{1,0:T(8,128)S(1)}, ...), condition=%wide.region_9.10_spmd.clone, body=%wide.region_7.9_spmd.clone.sunk | while | flops 338428544 | bytes 15370155 | solution.py:52
  90.9 1.8 fusion.27
  92.6 0.6 select_reduce_fusion.5
  93.3 0.3 select_maximum_fusion.5
  93.7 1.8 fusion.27
  95.5 0.6 select_reduce_fusion.5
  96.1 0.3 select_maximum_fusion.5
  96.6 1.8 fusion.27
  98.4 0.6 select_reduce_fusion.5
  99.5 1.8 fusion.27
  101.2 0.6 select_reduce_fusion.5
  102.3 1.8 fusion.27
  104.1 0.6 select_reduce_fusion.5
  105.2 1.8 fusion.27
  106.9 0.6 select_reduce_fusion.5
  108.0 1.8 fusion.27
  109.8 0.6 select_reduce_fusion.5
  110.9 1.8 fusion.27
  112.7 0.6 select_reduce_fusion.5
  113.3 0.3 select_maximum_fusion.5
  113.8 1.8 fusion.27
  115.5 0.6 select_reduce_fusion.5
  116.2 0.3 select_maximum_fusion.5
  116.5 1.3 copy.5
  117.9 59.8 %all-reduce.3.cloned.1.call-done = (f32[64,32,128]{2,1,0:T(8,128)}, f32[64,32,128]{2,1,0:T(8,128)}) async-done(((f32[64,32,128]{2,1,0:T(8,128)}, f32[64,32,128]{2,1,0:T(8,128)}), (f32[64,32,128]{2,1,0:T(8,128)}, f32[64,32,128]{2,1,0:T(8,128)})) %all-reduce.3.cloned.1.call-update) | async-done | bytes 2097168 | tf_op jit(solution)/shard_map/pmax | solution.py:57
  177.7 1.4 reduce_sum.39
  179.1 1.4 reduce_sum.38
  180.4 0.7 pad_maximum_fusion
  (52 shorter events, 3.6 us)
Async XLA Ops:
  6.5 8.6 %copy-start = (bf16[64,32,128]{2,1,0:T(8,128)(2,1)S(1)}, bf16[64,32,128]{2,1,0:T(8,128)(2,1)}, u32[]{:S(2)}) copy-start(bf16[64,32,128]{2,1,0:T(8,128)(2,1)} %param.7) | copy-start | bytes 1572868
  6.5 171.1 %all-reduce.3.cloned.1.call-start = ((), (), s32[]{:S(2)}) async-start(), calls=%async_computation | async-start | bytes 4194304 | tf_op jit(solution)/shard_map/pmax | solution.py:57
  11.8 41.9 %collective-permute-start = (bf16[45,128,128]{2,1,0:T(8,128)(2,1)}, bf16[45,128,128]{2,1,0:T(8,128)(2,1)}, u32[]{:S(2)}, u32[]{:S(2)}) collective-permute-start(bf16[45,128,128]{2,1,0:T(8,128)(2,1)} %fusion.10), channel_id=1, source_target_pairs={{252,0},{0,4},{4,8},{8,12},{12,16},{16,20},{20,24},{24,28},{28,32}... | collective-permute-start | bytes 4423688 | tf_op jit(solution)/shard_map/ppermute | solution.py:15
  53.7 37.1 %collective-permute-start.1 = (bf16[45,128,128]{2,1,0:T(8,128)(2,1)}, bf16[45,128,128]{2,1,0:T(8,128)(2,1)}, u32[]{:S(2)}, u32[]{:S(2)}) collective-permute-start(bf16[45,128,128]{2,1,0:T(8,128)(2,1)} %collective-permute-done), channel_id=1, source_target_pairs={{252,0},{0,4},{4,8},{8,12},{12,16},{16,20},{20,24},{24,28},{28,32}... | collective-permute-start | bytes 4423688 | tf_op jit(solution)/shard_map/ppermute | solution.py:15
Sparse Core Ops, SparseCore 0:
  118.0 59.6 all-reduce.2
where the time goes:
time: 189 us; the launch traced here: 188 us
  waiting for transfers between devices  108 us (57%)
  matrix products  31.6 us (17%)
  other arithmetic  28.2 us (15%)
  between operations  13.4 us (7%)
  local copies, waits for them, and re-layouts  3.61 us (2%)
  starting transfers between devices  2.47 us (1%)
    pmax x1, waiting for transfers between devices, combine(): merged = lax.pmax(maxima, 'tok')  59.8 us
    ppermute x2, waiting for transfers between devices, shifted(): return lax.ppermute(block, axis, route)  48 us
    dot_general x18, matrix products, one_group(): lax.dot_general(flat_q, doc_tile, (((1,), (1,)), ((), ())), preferred_ele...  31.6 us
    reduce_max x18, other arithmetic, one_group(): return (jnp.maximum(running, jnp.max(similar, axis=1)), None)  11.4 us
    max x18, other arithmetic, one_group(): return (jnp.maximum(running, jnp.max(similar, axis=1)), None)  6.16 us
  transfers between devices with their start and end apart: 3, of which 3 were waited for; matrix products, arithmetic and copies ran while one was open for 15% of the time, Pallas kernels for 0%

commit v1 on v0

v1 whole, which is shorter than its diff:
```python
import functools

import jax
import jax.numpy as jnp
from jax import lax
from jax.experimental import pallas as pl
from jax.experimental.pallas import tpu as pltpu
from jax.sharding import PartitionSpec as P

STEPS = 2
NEGATIVE_FILL = -1e30
GROUP = 8
SLOT_BLOCK = 16
COLUMNS = 256
VMEM_LIMIT = 40 * 1024 * 1024


def normalized(values):
    wide = values.astype(jnp.float32)
    return wide * lax.rsqrt(jnp.sum(wide * wide, axis=-1, keepdims=True) + 1e-06)


def arrange_queries(half_refs, core, wide_ref, q_ref):
    per_half, tokens, _ = half_refs[0].shape
    stride = 2 * STEPS * per_half
    for place, half_ref in enumerate(half_refs):
        step_no, other = place // 2, place % 2
        half = core if other == 0 else 1 - core

        def norm_one(i, carry, half_ref=half_ref):
            rows = pl.ds(pl.multiple_of(i * tokens, tokens), tokens)
            wide_ref[rows, :] = normalized(half_ref[i])
            return carry

        lax.fori_loop(0, per_half, norm_one, 0, unroll=8)

        def place_token(k, carry, step_no=step_no, half=half):
            first = k * stride + step_no * 2 * per_half + half * per_half
            rows = wide_ref[pl.ds(k, per_half, stride=tokens), :]
            q_ref[pl.ds(pl.multiple_of(first, per_half), per_half), :] = rows.astype(q_ref.dtype)
            return carry

        lax.fori_loop(0, tokens, place_token, 0, unroll=8)


def score_slab(slab_ref, base, order_ref, lens_ref, lens_wide_ref, q_ref, wide_ref, packed_ref, best_ref):
    docs, slots, _ = slab_ref.shape
    padded = -(-slots // SLOT_BLOCK) * SLOT_BLOCK
    blocks = padded // SLOT_BLOCK
    slot = lax.broadcasted_iota(jnp.int32, (slots, 1), 0)

    def norm_one(p, carry):
        rows = normalized(slab_ref[order_ref[p]])
        first = rows[0:1]
        rows = jnp.where(slot < lens_ref[p] - base, rows, first)
        rows = jnp.concatenate([rows, jnp.broadcast_to(first, (padded - slots, first.shape[1]))], axis=0)
        wide_ref[pl.ds(pl.multiple_of(p * padded, padded), padded), :] = rows
        return carry

    used = jnp.int32(0)
    for p in range(docs):
        used = used + (lens_ref[p] > base).astype(jnp.int32)
    groups = (used + GROUP - 1) // GROUP
    lax.fori_loop(0, groups * (GROUP // 4), lambda i, c: lax.fori_loop(0, 4, lambda k, d: norm_one(i * 4 + k, d), c, unroll=True), 0)

    def one_group(g, carry):
        start = g * GROUP * padded
        longest = lens_ref[g * GROUP] - base
        count = jnp.minimum((longest + SLOT_BLOCK - 1) // SLOT_BLOCK, blocks)

        def pack(i, c):
            for k in range(0, SLOT_BLOCK, 2):
                u = i * SLOT_BLOCK + k
                pair = [wide_ref[pl.ds(start + u + e, GROUP, stride=padded), :] for e in range(2)]
                rows = pl.ds(pl.multiple_of(u * GROUP, 2 * GROUP), 2 * GROUP)
                packed_ref[rows, :] = jnp.concatenate(pair, axis=0).astype(packed_ref.dtype)
            return c

        lax.fori_loop(0, count, pack, 0)
        rows_g = pl.ds(pl.multiple_of(g * GROUP, GROUP), GROUP)
        real = lens_wide_ref[rows_g, :][:, 0:1] > base
        for blocks_now in range(1, blocks + 1):

            @pl.when(count == blocks_now)
            def _():
                height = blocks_now * SLOT_BLOCK
                rows = packed_ref[0 : height * GROUP, :]
                for n in range(0, q_ref.shape[0], COLUMNS):
                    similar = lax.dot_general(
                        rows, q_ref[n : n + COLUMNS, :], (((1,), (1,)), ((), ())), preferred_element_type=jnp.float32
                    )
                    top = jnp.max(similar.reshape(height, GROUP, COLUMNS), axis=0)
                    top = jnp.where(real, top, NEGATIVE_FILL)
                    best_ref[rows_g, n : n + COLUMNS] = jnp.maximum(best_ref[rows_g, n : n + COLUMNS], top)

        return carry

    lax.fori_loop(0, groups, one_group, 0)


def early_kernel(where_ref, order_ref, lens_ref, lens_wide_ref, q0, q1, q2, q3, own_ref, near_ref, q_ref, best_ref, qwide_ref, wide_ref, packed_ref):
    tok = where_ref[0]
    slots = own_ref.shape[1]
    arrange_queries((q0, q1, q2, q3), lax.rem(tok, 2), qwide_ref, q_ref)
    best_ref[...] = jnp.full(best_ref.shape, NEGATIVE_FILL, jnp.float32)
    for k, slab_ref in enumerate((own_ref, near_ref)):
        base = (tok ^ k) * slots
        score_slab(slab_ref, base, order_ref, lens_ref, lens_wide_ref, q_ref, wide_ref, packed_ref, best_ref)


def late_kernel(where_ref, order_ref, lens_ref, lens_wide_ref, q_ref, early_ref, far_ref, far_other_ref, out_ref, best_ref, wide_ref, packed_ref, sums_ref):
    tok = where_ref[0]
    slots = far_ref.shape[1]
    best_ref[...] = early_ref[...]
    for k, slab_ref in ((2, far_ref), (3, far_other_ref)):
        base = (tok ^ k) * slots
        score_slab(slab_ref, base, order_ref, lens_ref, lens_wide_ref, q_ref, wide_ref, packed_ref, best_ref)
    docs, lanes = out_ref.shape
    total = best_ref[:, 0:lanes]
    for k in range(lanes, best_ref.shape[1], lanes):
        total = total + best_ref[:, k : k + lanes]
    sums_ref[...] = total

    def unsort(p, carry):
        out_ref[pl.ds(order_ref[p], 1), :] = sums_ref[pl.ds(p, 1), :]
        return carry

    lax.fori_loop(0, docs, unsort, 0, unroll=8)


SMEM = pl.BlockSpec(memory_space=pltpu.SMEM)
VMEM = pl.BlockSpec(memory_space=pltpu.VMEM)


def shifted(block, axis, distance):
    size = lax.axis_size(axis)
    return lax.ppermute(block, axis, [(i, (i + distance) % size) for i in range(size)])


def swapped(block, mask):
    return lax.ppermute(block, "tok", [(i, i ^ mask) for i in range(lax.axis_size("tok"))])


def per_device(queries, documents, lengths):
    qcount, tokens, width = queries.shape
    dcount, slots, _ = documents.shape
    tok_size = lax.axis_size("tok")
    tok, dp = lax.axis_index("tok"), lax.axis_index("dp")
    mine = dcount // tok_size
    q_rows = STEPS * qcount * tokens
    lanes = STEPS * qcount
    padded = -(-slots // SLOT_BLOCK) * SLOT_BLOCK

    half = lax.dynamic_slice_in_dim(queries, tok % 2 * (qcount // 2), qcount // 2, 0)
    slabs = [lax.dynamic_slice_in_dim(documents, (tok ^ k) * mine, mine, 0) for k in range(tok_size)]
    arrived = [shifted(half, "dp", -1 - s) for s in range(STEPS)]
    far = [swapped(slabs[k], k) for k in (2, 3)]
    near = swapped(slabs[1], 1)
    halves = []
    for block in arrived:
        halves += [block, swapped(block, 1)]

    lens = lax.dynamic_slice_in_dim(lengths, dp * dcount + tok * mine, mine, 0)
    index = jnp.arange(mine, dtype=jnp.int32)
    ahead = (lens[None, :] > lens[:, None]) | ((lens[None, :] == lens[:, None]) & (index[None, :] < index[:, None]))
    rank = jnp.sum(ahead.astype(jnp.int32), axis=1)
    at = rank[None, :] == index[:, None]
    order = jnp.sum(jnp.where(at, index[None, :], 0), axis=1)
    lens_sorted = jnp.sum(jnp.where(at, lens[None, :], 0), axis=1)
    lens_wide = jnp.broadcast_to(lens_sorted[:, None], (mine, 128))
    where = tok[None].astype(jnp.int32)

    slab_scratch = [
        pltpu.VMEM((mine * padded, width), jnp.float32),
        pltpu.VMEM((GROUP * padded, width), jnp.bfloat16),
    ]
    work = 2 * q_rows * mine * slots * width * 2
    params = pltpu.CompilerParams(vmem_limit_bytes=VMEM_LIMIT)
    q_all, early = pl.pallas_call(
        early_kernel,
        out_shape=(
            jax.ShapeDtypeStruct((q_rows, width), jnp.bfloat16),
            jax.ShapeDtypeStruct((mine, q_rows), jnp.float32),
        ),
        in_specs=[SMEM] * 3 + [VMEM] * 7,
        out_specs=(VMEM, VMEM),
        scratch_shapes=[pltpu.VMEM((qcount // 2 * tokens, width), jnp.float32)] + slab_scratch,
        compiler_params=params,
        cost_estimate=pl.CostEstimate(flops=work, bytes_accessed=1 << 22, transcendentals=0),
        name="early",
    )(where, order, lens_sorted, lens_wide, *halves, slabs[0], near)
    scores = pl.pallas_call(
        late_kernel,
        out_shape=jax.ShapeDtypeStruct((mine, lanes), jnp.float32),
        in_specs=[SMEM] * 3 + [VMEM] * 5,
        out_specs=VMEM,
        scratch_shapes=[pltpu.VMEM((mine, q_rows), jnp.float32)] + slab_scratch + [pltpu.VMEM((mine, lanes), jnp.float32)],
        compiler_params=params,
        cost_estimate=pl.CostEstimate(flops=work, bytes_accessed=1 << 22, transcendentals=0),
        name="late",
    )(where, order, lens_sorted, lens_wide, q_all, early, *far)

    every = lax.all_gather(scores, "tok", axis=0, tiled=True)
    results = [shifted(every[:, s * qcount : (s + 1) * qcount], "dp", 1 + s) for s in range(STEPS)]
    return jnp.stack([block.T for block in results], axis=1)


def solution(mesh):
    in_specs = (P("dp", None, None), P("dp", "tok", None), P())
    out_specs = P("dp", None, None)
    return jax.shard_map(per_device, mesh=mesh, in_specs=in_specs, out_specs=out_specs, check_vma=False)
```

time: 189 us -> 79.3 us (0.42)
  waiting for transfers between devices: 108 us -> 21.5 us
  matrix products: 31.6 us -> 0 us
  other arithmetic: 28.2 us -> 0.31 us
  Pallas kernels: 0 us -> 18.3 us
  starting transfers between devices: 2.47 us -> 19.8 us
  between operations: 13.4 us -> 0.1 us
  blocking collectives: 0 us -> 12.5 us
  local copies, waits for them, and re-layouts: 3.61 us -> 6.37 us
    pmax x1 -> x0, waiting for transfers between devices: 59.8 us -> none  [combine(): merged = lax.pmax(maxima, 'tok')]
    dot_general x18 -> x0, matrix products: 31.6 us -> none  [one_group(): lax.dot_general(flat_q, doc_tile, (((1,), (1,)), ((), ())), preferred_ele...]
    ppermute x2 -> x9, waiting for transfers between devices: 48 us -> 21.5 us  [the longest x4 19.7 us: shifted(): lax.ppermute(block, axis, [(i, (i + distance) % size) for i in range(size)])]
    pallas_call x0 -> x2, Pallas kernels: none -> 18.3 us  [the longest x1 13.8 us: per_device(): pl.pallas_call(early_kernel, out_shape=(jax.ShapeDtypeStruct((q_rows, wid...]
    ppermute x2 -> x9, starting transfers between devices: 2.47 us -> 19.8 us  [the longest x4 11 us: shifted(): lax.ppermute(block, axis, [(i, (i + distance) % size) for i in range(size)])]
    all_gather x0 -> x1, blocking collectives: none -> 12.5 us  [per_device(): every = lax.all_gather(scores, 'tok', axis=0, tiled=True)]
    reduce_max x18 -> x0, other arithmetic: 11.4 us -> none  [one_group(): return (jnp.maximum(running, jnp.max(similar, axis=1)), None)]
    max x18 -> x0, other arithmetic: 6.16 us -> none  [one_group(): return (jnp.maximum(running, jnp.max(similar, axis=1)), None)]
  transfers between devices with their start and end apart: 3 -> 9, of which waited for: 3 -> 5; matrix products, arithmetic and copies ran while one was open for 15% -> 6% of each run, Pallas kernels for 0% -> 17%
where the time goes in v1:
time: 79.3 us; the launch traced here: 79 us
  waiting for transfers between devices  21.5 us (27%)
  starting transfers between devices  19.8 us (25%)
  Pallas kernels  18.3 us (23%)
  blocking collectives  12.5 us (16%)
  local copies, waits for them, and re-layouts  6.37 us (8%)
    ppermute x4, waiting for transfers between devices, shifted(): lax.ppermute(block, axis, [(i, (i + distance) % size) for i in range(size)])  19.7 us
    pallas_call x1, Pallas kernels, per_device(): pl.pallas_call(early_kernel, out_shape=(jax.ShapeDtypeStruct((q_rows, wid...  13.8 us
    all_gather x1, blocking collectives, per_device(): every = lax.all_gather(scores, 'tok', axis=0, tiled=True)  12.5 us
    ppermute x4, starting transfers between devices, shifted(): lax.ppermute(block, axis, [(i, (i + distance) % size) for i in range(size)])  11 us
    ppermute x5, starting transfers between devices, swapped(): lax.ppermute(block, 'tok', [(i, i ^ mask) for i in range(lax.axis_size('t...  8.84 us
    pallas_call x1, Pallas kernels, per_device(): pl.pallas_call(late_kernel, out_shape=jax.ShapeDtypeStruct((mine, lanes),...  4.56 us
    unnamed x6, local copies, waits for them, and re-layouts  3.13 us
    ppermute x5, waiting for transfers between devices, swapped(): lax.ppermute(block, 'tok', [(i, i ^ mask) for i in range(lax.axis_size('t...  1.85 us
  transfers between devices with their start and end apart: 9, of which 5 were waited for; matrix products, arithmetic and copies ran while one was open for 6% of the time, Pallas kernels for 17%

profile of v1, /device:TPU:1, one launch (start us, length us, event | category | flops | bytes accessed | tf_op | source)
XLA Modules:
  0.0 79.0 jit_solution(18188268348493979999)
XLA Ops:
  0.0 0.0 copy-start
  0.0 1.0 %copy-done = bf16[64,32,128]{2,1,0:T(8,128)(2,1)S(1)} copy-done((bf16[64,32,128]{2,1,0:T(8,128)(2,1)S(1)}, bf16[64,32,128]{2,1,0:T(8,128)(2,1)}, u32[]{:S(2)}) %copy-start) | copy-done | bytes 524312
  1.1 9.7 %collective-permute-start = (bf16[32,32,128]{2,1,0:T(8,128)(2,1)S(1)}, bf16[32,32,128]{2,1,0:T(8,128)(2,1)S(1)}, u32[]{:S(2)}, u32[]{:S(2)}) collective-permute-start(bf16[32,32,128]{2,1,0:T(8,128)(2,1)S(1)} %constant_dynamic-slice_fusion.3), channel_id=1, source_target_pairs={{0,252},{4,0},{8,4},{12,8},{16,12},{20,16},{24,20},{28,24},{32,28}... | collective-permute-start | bytes 786440 | tf_op jit(solution)/shard_map/ppermute | solution.py:137
  10.8 1.2 %collective-permute-start.2 = (bf16[32,32,128]{2,1,0:T(8,128)(2,1)S(1)}, bf16[32,32,128]{2,1,0:T(8,128)(2,1)S(1)}, u32[]{:S(2)}, u32[]{:S(2)}) collective-permute-start(bf16[32,32,128]{2,1,0:T(8,128)(2,1)S(1)} %constant_dynamic-slice_fusion.3), channel_id=1, source_target_pairs={{0,248},{4,252},{8,0},{12,4},{16,8},{20,12},{24,16},{28,20},{32,24... | collective-permute-start | bytes 786440 | tf_op jit(solution)/shard_map/ppermute | solution.py:137
  11.9 1.6 %constant_dynamic-slice_fusion.4 = (bf16[32,45,128]{2,0,1:T(8,128)(2,1)S(1)}, bf16[32,45,128]{2,0,1:T(8,128)(2,1)S(1)}, bf16[32,45,128]{2,0,1:T(8,128)(2,1)S(1)}, bf16[32,45,128]{2,0,1:T(8,128)(2,1)S(1)}) fusion(bf16[128,45,128]{2,0,1:T(8,128)(2,1)} %param.4, s32[]{:T(128)S(6)} %select_n.40, s32[]{:T(128)S(6)} %select_n.39, s32[]{:T(128)S(6)} %select_n.38, ...), kind=kLoop, calls=%fused_computation.12 | loop fusion | bytes 2949136 | tf_op jit(solution)/shard_map/dynamic_slice | solution.py:155
  13.5 0.2 copy.15
  13.7 1.3 %collective-permute-start.4 = (bf16[32,45,128]{2,1,0:T(8,128)(2,1)S(1)}, bf16[32,45,128]{2,1,0:T(8,128)(2,1)S(1)}, u32[]{:S(2)}, u32[]{:S(2)}) collective-permute-start(bf16[32,45,128]{2,1,0:T(8,128)(2,1)S(1)} %copy.15), channel_id=1, source_target_pairs={{0,1},{1,0},{2,3},{3,2},{4,5},{5,4},{6,7},{7,6},{8,9},{9,8},{10,11... | collective-permute-start | bytes 1105928 | tf_op jit(solution)/shard_map/ppermute | solution.py:141
  15.0 5.6 %collective-permute-done.q0 = bf16[32,32,128]{2,1,0:T(8,128)(2,1)S(1)} collective-permute-done((bf16[32,32,128]{2,1,0:T(8,128)(2,1)S(1)}, bf16[32,32,128]{2,1,0:T(8,128)(2,1)S(1)}, u32[]{:S(2)}, u32[]{:S(2)}) %collective-permute-start) | collective-permute-done | bytes 262176 | tf_op jit(solution)/shard_map/ppermute | solution.py:137
  20.6 2.8 %collective-permute-start.1 = (bf16[32,32,128]{2,1,0:T(8,128)(2,1)S(1)}, bf16[32,32,128]{2,1,0:T(8,128)(2,1)S(1)}, u32[]{:S(2)}, u32[]{:S(2)}) collective-permute-start(bf16[32,32,128]{2,1,0:T(8,128)(2,1)S(1)} %collective-permute-done.q0), channel_id=1, source_target_pairs={{0,1},{1,0},{2,3},{3,2},{4,5},{5,4},{6,7},{7,6},{8,9},{9,8},{10,11... | collective-permute-start | bytes 786440 | tf_op jit(solution)/shard_map/ppermute | solution.py:141
  23.4 3.5 %collective-permute-done.2.q2 = bf16[32,32,128]{2,1,0:T(8,128)(2,1)S(1)} collective-permute-done((bf16[32,32,128]{2,1,0:T(8,128)(2,1)S(1)}, bf16[32,32,128]{2,1,0:T(8,128)(2,1)S(1)}, u32[]{:S(2)}, u32[]{:S(2)}) %collective-permute-start.2) | collective-permute-done | bytes 262176 | tf_op jit(solution)/shard_map/ppermute | solution.py:137
  27.0 1.5 %collective-permute-start.3 = (bf16[32,32,128]{2,1,0:T(8,128)(2,1)S(1)}, bf16[32,32,128]{2,1,0:T(8,128)(2,1)S(1)}, u32[]{:S(2)}, u32[]{:S(2)}) collective-permute-start(bf16[32,32,128]{2,1,0:T(8,128)(2,1)S(1)} %collective-permute-done.2.q2), channel_id=1, source_target_pairs={{0,1},{1,0},{2,3},{3,2},{4,5},{5,4},{6,7},{7,6},{8,9},{9,8},{10,11... | collective-permute-start | bytes 786440 | tf_op jit(solution)/shard_map/ppermute | solution.py:141
  28.5 0.9 %copy.16 = bf16[32,45,128]{2,1,0:T(8,128)(2,1)} copy(bf16[32,45,128]{2,0,1:T(8,128)(2,1)S(1)} %get-tuple-element.12) | data formatting | bytes 737280
  29.4 2.6 %collective-permute-start.5 = (bf16[32,45,128]{2,1,0:T(8,128)(2,1)}, bf16[32,45,128]{2,1,0:T(8,128)(2,1)S(1)}, u32[]{:S(2)}, u32[]{:S(2)}) collective-permute-start(bf16[32,45,128]{2,1,0:T(8,128)(2,1)} %copy.16), channel_id=1, source_target_pairs={{0,2},{1,3},{2,0},{3,1},{4,6},{5,7},{6,4},{7,5},{8,10},{9,11},{10,... | collective-permute-start | bytes 1105928 | tf_op jit(solution)/shard_map/ppermute | solution.py:141
  32.0 0.9 %copy.17 = bf16[32,45,128]{2,1,0:T(8,128)(2,1)} copy(bf16[32,45,128]{2,0,1:T(8,128)(2,1)S(1)} %get-tuple-element.11) | data formatting | bytes 737280
  32.9 0.5 collective-permute-start.6
  33.4 0.1 copy.14.own_ref
  33.6 0.8 dynamic_slice.18
  34.4 0.2 convert_reduce_fusion
  34.6 0.1 select_reduce_fusion
  34.7 0.0 collective-permute-done.4.near_ref
  34.7 0.0 collective-permute-done.1.q1
  34.7 0.0 collective-permute-done.3.q3
  34.7 0.1 broadcast_in_dim.20.lens_wide_ref
  34.8 13.8 %early.1 = (bf16[4096,128]{1,0:T(8,128)(2,1)S(1)}, f32[32,4096]{1,0:T(8,128)S(1)}) custom-call(s32[1]{0:T(128)} %bitcast.where_ref, s32[32]{0:T(128)S(1)} %get-tuple-element.10.order_ref, s32[32]{0:T(128)S(1)} %get-tuple-element.9.lens_ref, s32[32,128]{1,0:T(8,128)S(1)} %broadcast_in_dim.20.lens_wide_ref, bf16[32,32,128]{2,1,0:T(8,128)(2,1)S(1)} %collective-permute-done.q0, ...), custom_call_target="tpu_custom_call" | custom-call | flops 3019898880 | bytes 4194304 | tf_op jit(solution)/shard_map/early/pallas_call | solution.py:179
  48.5 0.0 collective-permute-done.5.far_ref
  48.5 1.8 %collective-permute-done.6.far_other_ref = bf16[32,45,128]{2,1,0:T(8,128)(2,1)S(1)} collective-permute-done((bf16[32,45,128]{2,1,0:T(8,128)(2,1)}, bf16[32,45,128]{2,1,0:T(8,128)(2,1)S(1)}, u32[]{:S(2)}, u32[]{:S(2)}) %collective-permute-start.6) | collective-permute-done | bytes 368672 | tf_op jit(solution)/shard_map/ppermute | solution.py:141
  50.4 4.6 %late.1 = f32[32,128]{1,0:T(8,128)S(1)} custom-call(s32[1]{0:T(128)} %bitcast.where_ref, s32[32]{0:T(128)S(1)} %get-tuple-element.10.order_ref, s32[32]{0:T(128)S(1)} %get-tuple-element.9.lens_ref, s32[32,128]{1,0:T(8,128)S(1)} %broadcast_in_dim.20.lens_wide_ref, bf16[4096,128]{1,0:T(8,128)(2,1)S(1)} %get-tuple-element.7.q_ref, ...), custom_call_target="tpu_custom_call" | custom-call | flops 3019898880 | bytes 4194304 | tf_op jit(solution)/shard_map/late/pallas_call | solution.py:192
  55.0 12.5 %all_gather.3 = f32[128,128]{1,0:T(8,128)S(1)} all-gather(f32[32,128]{1,0:T(8,128)S(1)} %late.1), channel_id=1, replica_groups=mesh['dp'=64,'tok'=4] {'tok'}, dimensions={0}, use_global_device_ids=true | all-gather | bytes 81920 | tf_op jit(solution)/shard_map/all_gather | solution.py:203
  67.5 0.1 fusion.2
  67.6 0.1 collective-permute-start.7
  67.6 0.1 collective-permute-start.8
  67.7 7.6 %collective-permute-done.7 = f32[128,64]{1,0:T(8,128)S(1)} collective-permute-done((f32[128,64]{1,0:T(8,128)S(1)}, f32[128,64]{1,0:T(8,128)S(1)}, u32[]{:S(2)}, u32[]{:S(2)}) %collective-permute-start.7) | collective-permute-done | bytes 32800 | tf_op jit(solution)/shard_map/ppermute | solution.py:137
  75.4 2.9 %collective-permute-done.8 = f32[128,64]{1,0:T(8,128)S(1)} collective-permute-done((f32[128,64]{1,0:T(8,128)S(1)}, f32[128,64]{1,0:T(8,128)S(1)}, u32[]{:S(2)}, u32[]{:S(2)}) %collective-permute-start.8) | collective-permute-done | bytes 32800 | tf_op jit(solution)/shard_map/ppermute | solution.py:137
  78.3 0.7 copy.13
  (2 shorter events, 0.0 us)
Async XLA Ops:
  0.0 1.0 %copy-start = (bf16[64,32,128]{2,1,0:T(8,128)(2,1)S(1)}, bf16[64,32,128]{2,1,0:T(8,128)(2,1)}, u32[]{:S(2)}) copy-start(bf16[64,32,128]{2,1,0:T(8,128)(2,1)} %param.3) | copy-start | bytes 1572868
  1.1 19.5 %collective-permute-start = (bf16[32,32,128]{2,1,0:T(8,128)(2,1)S(1)}, bf16[32,32,128]{2,1,0:T(8,128)(2,1)S(1)}, u32[]{:S(2)}, u32[]{:S(2)}) collective-permute-start(bf16[32,32,128]{2,1,0:T(8,128)(2,1)S(1)} %constant_dynamic-slice_fusion.3), channel_id=1, source_target_pairs={{0,252},{4,0},{8,4},{12,8},{16,12},{20,16},{24,20},{28,24},{32,28}... | collective-permute-start | bytes 786440 | tf_op jit(solution)/shard_map/ppermute | solution.py:137
  10.8 16.2 %collective-permute-start.2 = (bf16[32,32,128]{2,1,0:T(8,128)(2,1)S(1)}, bf16[32,32,128]{2,1,0:T(8,128)(2,1)S(1)}, u32[]{:S(2)}, u32[]{:S(2)}) collective-permute-start(bf16[32,32,128]{2,1,0:T(8,128)(2,1)S(1)} %constant_dynamic-slice_fusion.3), channel_id=1, source_target_pairs={{0,248},{4,252},{8,0},{12,4},{16,8},{20,12},{24,16},{28,20},{32,24... | collective-permute-start | bytes 786440 | tf_op jit(solution)/shard_map/ppermute | solution.py:137
  13.7 21.0 %collective-permute-start.4 = (bf16[32,45,128]{2,1,0:T(8,128)(2,1)S(1)}, bf16[32,45,128]{2,1,0:T(8,128)(2,1)S(1)}, u32[]{:S(2)}, u32[]{:S(2)}) collective-permute-start(bf16[32,45,128]{2,1,0:T(8,128)(2,1)S(1)} %copy.15), channel_id=1, source_target_pairs={{0,1},{1,0},{2,3},{3,2},{4,5},{5,4},{6,7},{7,6},{8,9},{9,8},{10,11... | collective-permute-start | bytes 1105928 | tf_op jit(solution)/shard_map/ppermute | solution.py:141
  20.6 14.1 %collective-permute-start.1 = (bf16[32,32,128]{2,1,0:T(8,128)(2,1)S(1)}, bf16[32,32,128]{2,1,0:T(8,128)(2,1)S(1)}, u32[]{:S(2)}, u32[]{:S(2)}) collective-permute-start(bf16[32,32,128]{2,1,0:T(8,128)(2,1)S(1)} %collective-permute-done.q0), channel_id=1, source_target_pairs={{0,1},{1,0},{2,3},{3,2},{4,5},{5,4},{6,7},{7,6},{8,9},{9,8},{10,11... | collective-permute-start | bytes 786440 | tf_op jit(solution)/shard_map/ppermute | solution.py:141
  27.0 7.7 %collective-permute-start.3 = (bf16[32,32,128]{2,1,0:T(8,128)(2,1)S(1)}, bf16[32,32,128]{2,1,0:T(8,128)(2,1)S(1)}, u32[]{:S(2)}, u32[]{:S(2)}) collective-permute-start(bf16[32,32,128]{2,1,0:T(8,128)(2,1)S(1)} %collective-permute-done.2.q2), channel_id=1, source_target_pairs={{0,1},{1,0},{2,3},{3,2},{4,5},{5,4},{6,7},{7,6},{8,9},{9,8},{10,11... | collective-permute-start | bytes 786440 | tf_op jit(solution)/shard_map/ppermute | solution.py:141
  29.4 19.1 %collective-permute-start.5 = (bf16[32,45,128]{2,1,0:T(8,128)(2,1)}, bf16[32,45,128]{2,1,0:T(8,128)(2,1)S(1)}, u32[]{:S(2)}, u32[]{:S(2)}) collective-permute-start(bf16[32,45,128]{2,1,0:T(8,128)(2,1)} %copy.16), channel_id=1, source_target_pairs={{0,2},{1,3},{2,0},{3,1},{4,6},{5,7},{6,4},{7,5},{8,10},{9,11},{10,... | collective-permute-start | bytes 1105928 | tf_op jit(solution)/shard_map/ppermute | solution.py:141
  32.9 17.5 %collective-permute-start.6 = (bf16[32,45,128]{2,1,0:T(8,128)(2,1)}, bf16[32,45,128]{2,1,0:T(8,128)(2,1)S(1)}, u32[]{:S(2)}, u32[]{:S(2)}) collective-permute-start(bf16[32,45,128]{2,1,0:T(8,128)(2,1)} %copy.17), channel_id=1, source_target_pairs={{0,3},{1,2},{2,1},{3,0},{4,7},{5,6},{6,5},{7,4},{8,11},{9,10},{10,... | collective-permute-start | bytes 1105928 | tf_op jit(solution)/shard_map/ppermute | solution.py:141
  67.6 7.8 %collective-permute-start.7 = (f32[128,64]{1,0:T(8,128)S(1)}, f32[128,64]{1,0:T(8,128)S(1)}, u32[]{:S(2)}, u32[]{:S(2)}) collective-permute-start(f32[128,64]{1,0:T(8,128)S(1)} %get-tuple-element.15), channel_id=1, source_target_pairs={{0,4},{4,8},{8,12},{12,16},{16,20},{20,24},{24,28},{28,32},{32,36}... | collective-permute-start | bytes 98312 | tf_op jit(solution)/shard_map/ppermute | solution.py:137
  67.6 10.6 %collective-permute-start.8 = (f32[128,64]{1,0:T(8,128)S(1)}, f32[128,64]{1,0:T(8,128)S(1)}, u32[]{:S(2)}, u32[]{:S(2)}) collective-permute-start(f32[128,64]{1,0:T(8,128)S(1)} %get-tuple-element.16), channel_id=1, source_target_pairs={{0,8},{4,12},{8,16},{12,20},{16,24},{20,28},{24,32},{28,36},{32,40... | collective-permute-start | bytes 98312 | tf_op jit(solution)/shard_map/ppermute | solution.py:137

commit v2 on v0

v2 whole, which is shorter than its diff:
```python
import functools

import jax
import jax.numpy as jnp
from jax import lax
from jax.experimental import pallas as pl
from jax.experimental.pallas import tpu as pltpu
from jax.sharding import PartitionSpec as P

STEPS = 2
NEGATIVE_FILL = -1e30
CHUNK = 16
GROUP = 8
BLOCK = CHUNK * GROUP
NARROW_GROUPS = 4
BATCH = 8
COLUMNS = 256
LANES = 128
VMEM_LIMIT = 40 * 1024 * 1024
SMEM = pl.BlockSpec(memory_space=pltpu.SMEM)
VMEM = pl.BlockSpec(memory_space=pltpu.VMEM)


def normalized(values):
    wide = values.astype(jnp.float32)
    return wide * lax.rsqrt(jnp.sum(wide * wide, axis=-1, keepdims=True) + 1e-06)


def chunks_of(slots):
    return -(-slots // CHUNK)


def prepare_kernel(half_ref, out_ref, wide_ref):
    count, tokens, _ = half_ref.shape

    def norm_one(i, carry):
        rows = pl.ds(pl.multiple_of(i * tokens, tokens), tokens)
        wide_ref[rows, :] = normalized(half_ref[i])
        return carry

    lax.fori_loop(0, count, norm_one, 0, unroll=16)

    def place_token(k, carry):
        out_ref[k] = wide_ref[pl.ds(k, count, stride=tokens), :].astype(out_ref.dtype)
        return carry

    lax.fori_loop(0, tokens, place_token, 0, unroll=16)


def pack(slab_ref, which, offset, info_ref, starts_ref, lens_ref, wide_ref, rows_ref):
    slots, docs, _ = slab_ref.shape
    chunks = chunks_of(slots)
    base = (info_ref[0] ^ which) * slots
    first = normalized(slab_ref[0])
    wide_ref[0:docs, :] = first
    for u in range(slots, chunks * CHUNK):
        wide_ref[u * docs : (u + 1) * docs, :] = first

    def norm_one(u, carry):
        rows = pl.ds(pl.multiple_of(u * docs, docs), docs)
        wide_ref[rows, :] = jnp.where(u + base < lens_ref[...], normalized(slab_ref[u]), first)
        return carry

    lax.fori_loop(1, slots, norm_one, 0, unroll=True)

    def place_one(j, carry):
        start = starts_ref[which * docs + j] - offset
        for c in range(chunks):
            at = start + c
            group = at // GROUP
            rows = wide_ref[pl.ds(c * CHUNK * docs + j, CHUNK, stride=docs), :]
            rows_ref[pl.ds(group * BLOCK + at - group * GROUP, CHUNK, stride=GROUP), :] = rows
        return carry

    lax.fori_loop(0, docs, place_one, 0, unroll=16)


def narrow(rows_ref, packed_ref, count, shift=0):
    size = NARROW_GROUPS * BLOCK

    def one(s, carry):
        source = pl.ds(pl.multiple_of(s * size, size), size)
        target = pl.ds(pl.multiple_of(s * size + shift * BLOCK, BLOCK), size)
        packed_ref[target, :] = rows_ref[source, :].astype(packed_ref.dtype)
        return carry

    lax.fori_loop(0, (count + NARROW_GROUPS - 1) // NARROW_GROUPS, one, 0)


def multiply(packed_ref, first, count, q_refs, top_ref):
    tokens, queries, width = q_refs[0].shape
    tiles = len(q_refs) * tokens * queries // LANES
    step = COLUMNS // queries

    def run(s, groups):
        rows = packed_ref[pl.ds(pl.multiple_of(s * BLOCK, BLOCK), groups * BLOCK), :]
        tile = 0
        for q_ref in q_refs:
            for k in range(0, tokens, step):
                q = q_ref[k : k + step].reshape(COLUMNS, width)
                similar = lax.dot_general(rows, q, (((1,), (1,)), ((), ())), preferred_element_type=jnp.float32)
                top = jnp.max(similar.reshape(groups, CHUNK, GROUP, COLUMNS), axis=1)
                for e in range(0, COLUMNS, LANES):
                    for b in range(groups):
                        place = pl.ds((s + b) * GROUP * tiles + tile, GROUP, stride=tiles)
                        top_ref[place, :] = top[b, :, e : e + LANES]
                    tile += 1

    whole = count // BATCH

    def batch(i, carry):
        run(first + i * BATCH, BATCH)
        return carry

    lax.fori_loop(0, whole, batch, 0)
    size = BATCH // 2
    while size:
        done = count // (2 * size) * (2 * size)

        @pl.when(count - done >= size)
        def _(size=size, done=done):
            run(first + done, size)

        size //= 2


def combine(top_ref, lists, offset, starts_ref, counts_ref, old_ref, best_ref, chunks):
    docs = starts_ref.shape[0] // 4
    tiles = best_ref.shape[0] // docs

    def one(j, carry):
        rows = pl.ds(pl.multiple_of(j * tiles, tiles), tiles)
        best = jnp.full((tiles, LANES), NEGATIVE_FILL, jnp.float32) if old_ref is None else old_ref[rows, :]
        for which in lists:
            start = starts_ref[which * docs + j] - offset
            count = counts_ref[which * docs + j]
            for c in range(chunks):
                top = top_ref[pl.ds(pl.multiple_of((start + c) * tiles, tiles), tiles), :]
                best = jnp.maximum(best, jnp.where(c < count, top, NEGATIVE_FILL))
        best_ref[rows, :] = best
        return carry

    lax.fori_loop(0, docs, one, 0, unroll=16)


def pack_kernel(info, starts, lens, own, near, packed_ref, wide_ref, rows_ref):
    pack(own, 0, 0, info, starts, lens, wide_ref, rows_ref)
    pack(near, 1, 0, info, starts, lens, wide_ref, rows_ref)
    narrow(rows_ref, packed_ref, info[3])


def early_kernel(info, starts, counts, packed, qa, qb, best_ref, top_ref, *, chunks):
    multiply(packed, 0, info[3], (qa, qb), top_ref)
    combine(top_ref, (0, 1), 0, starts, counts, None, best_ref, chunks)


def middle_kernel(info, starts, counts, lens, far, qa, qb, old, packed_ref, best_ref, wide_ref, rows_ref, top_ref):
    offset = info[3] * GROUP
    pack(far, 2, offset, info, starts, lens, wide_ref, rows_ref)
    groups = info[4] - info[3]
    narrow(rows_ref, packed_ref, groups)
    multiply(packed_ref, 0, groups, (qa, qb), top_ref)
    combine(top_ref, (2,), offset, starts, counts, old, best_ref, chunks_of(far.shape[0]))


def token_sums(best_ref, first, docs, tiles, per_half, count):
    total = best_ref[pl.ds(first, docs, stride=tiles), :]
    for k in range(first + 1, first + per_half):
        total = total + best_ref[pl.ds(k, docs, stride=tiles), :]
    shift = LANES // 2
    while shift >= count:
        total = total + pltpu.roll(total, shift, 1)
        shift //= 2
    return total


def query_sums(best_ref, step_no, tok, docs, count):
    tiles = best_ref.shape[0] // docs
    half = lax.rem(tok, 2)
    lane_group = lax.broadcasted_iota(jnp.int32, (docs, LANES), 1) // count
    merged = jnp.zeros((docs, LANES), jnp.float32)
    for other in range(2):
        part = token_sums(best_ref, other * (tiles // 2), docs, tiles, tiles // 2, count)
        place = 2 * step_no + (half if other == 0 else 1 - half)
        merged = jnp.where(lane_group == place, part, merged)
    return merged


def last_slab_kernel(
    info, starts, counts, lens, far, near_packed, far_packed, qa, qb, old, packed_ref, sums_ref,
    best_ref, wide_ref, rows_ref, top_ref,
):
    slots, docs, _ = far.shape
    narrow(near_packed, packed_ref, info[3])
    narrow(far_packed, packed_ref, info[4] - info[3], info[3])
    pack(far, 3, info[4] * GROUP, info, starts, lens, wide_ref, rows_ref)
    narrow(rows_ref, packed_ref, info[5] - info[4], info[4])
    multiply(packed_ref, info[4], info[5] - info[4], (qa, qb), top_ref)
    combine(top_ref, (3,), 0, starts, counts, old, best_ref, chunks_of(slots))
    sums_ref[...] = query_sums(best_ref, 0, info[0], docs, qa.shape[1])


def late_kernel(info, starts, counts, packed, qa, qb, sums, out_ref, best_ref, top_ref, *, chunks):
    docs = sums.shape[0]
    multiply(packed, 0, info[5], (qa, qb), top_ref)
    combine(top_ref, (0, 1, 2, 3), 0, starts, counts, None, best_ref, chunks)
    out_ref[...] = sums[...] + query_sums(best_ref, 1, info[0], docs, qa.shape[1])


def shifted(block, axis, distance):
    size = lax.axis_size(axis)
    return lax.ppermute(block, axis, [(i, (i + distance) % size) for i in range(size)])


def swapped(block, mask):
    return lax.ppermute(block, "tok", [(i, i ^ mask) for i in range(lax.axis_size("tok"))])


def returned(block, mask):
    dp_size, tok_size = lax.axis_size("dp"), lax.axis_size("tok")
    route = [
        (i * tok_size + t, (i + 1 + t % 2) % dp_size * tok_size + (t ^ mask))
        for i in range(dp_size)
        for t in range(tok_size)
    ]
    return lax.ppermute(block, ("dp", "tok"), route)


def in_order(own, other, own_first):
    return jnp.where(own_first, jnp.concatenate([own, other], axis=0), jnp.concatenate([other, own], axis=0))


def per_device(queries, documents, lengths):
    qcount, tokens, width = queries.shape
    dcount, slots, _ = documents.shape
    tok_size = lax.axis_size("tok")
    tok, dp = lax.axis_index("tok"), lax.axis_index("dp")
    core = tok % 2
    mine = dcount // tok_size
    half = qcount // 2
    tiles = qcount * tokens // LANES
    chunks = chunks_of(slots)
    list_rows = mine * chunks * CHUNK
    spare = NARROW_GROUPS * BLOCK
    params = pltpu.CompilerParams(vmem_limit_bytes=VMEM_LIMIT)
    cost = pl.CostEstimate(flops=1 << 10, bytes_accessed=1 << 10, transcendentals=0)
    bf16, f32 = jnp.bfloat16, jnp.float32

    by_slot = jnp.transpose(documents, (1, 0, 2))
    slabs = [lax.dynamic_slice_in_dim(by_slot, (tok ^ k) * mine, mine, 1) for k in range(tok_size)]
    prepared = pl.pallas_call(
        prepare_kernel,
        out_shape=jax.ShapeDtypeStruct((tokens, half, width), bf16),
        in_specs=[VMEM],
        out_specs=VMEM,
        scratch_shapes=[pltpu.VMEM((half * tokens, width), f32)],
        compiler_params=params,
        cost_estimate=cost,
        name="prepare",
    )(lax.dynamic_slice_in_dim(queries, core * half, half, 0))
    arrived = shifted(prepared, "dp", -1)
    far = swapped(slabs[2], 2)
    far_other = swapped(slabs[3], 3)
    near = swapped(slabs[1], 1)

    lens = lax.dynamic_slice_in_dim(lengths, dp * dcount + tok * mine, mine, 0)
    bases = (tok ^ jnp.arange(tok_size, dtype=jnp.int32)) * slots
    counts = jnp.clip((lens[None, :] - bases[:, None] + CHUNK - 1) // CHUNK, 0, chunks)
    index = jnp.arange(mine)
    before = jnp.sum(jnp.where(index[None, None, :] < index[None, :, None], counts[:, None, :], 0), axis=2)
    groups = (jnp.sum(counts, axis=1) + GROUP - 1) // GROUP
    which = jnp.arange(tok_size + 1)
    ends = jnp.sum(jnp.where(which[None, :tok_size] < which[:, None], groups[None, :], 0), axis=1)
    starts = before + ends[:tok_size, None] * GROUP
    info = jnp.concatenate([tok[None], ends]).astype(jnp.int32)
    wide_lens = jnp.broadcast_to(lens[:, None], (mine, LANES))
    starts, counts = starts.reshape(-1), counts.reshape(-1)

    def scratch(lists):
        return [
            pltpu.VMEM((mine * chunks * CHUNK, width), f32),
            pltpu.VMEM((lists * list_rows + spare, width), f32),
        ]

    def tops(lists):
        return pltpu.VMEM((lists * mine * chunks * tiles + 2 * GROUP * tiles, LANES), f32)

    best_shape = jax.ShapeDtypeStruct((mine * tiles, LANES), f32)
    best_scratch = pltpu.VMEM((mine * tiles, LANES), f32)

    def call(kernel, name, out_shape, scratch_shapes, *operands):
        scalar_count = 3 if kernel is not pack_kernel else 2
        return pl.pallas_call(
            kernel,
            out_shape=out_shape,
            in_specs=[SMEM] * scalar_count + [VMEM] * (len(operands) - scalar_count),
            out_specs=jax.tree.map(lambda _: VMEM, out_shape),
            scratch_shapes=scratch_shapes,
            compiler_params=params,
            cost_estimate=cost,
            name=name,
        )(*operands)

    near_packed = call(
        pack_kernel, "pack_near", jax.ShapeDtypeStruct((2 * list_rows + spare, width), bf16), scratch(2),
        info, starts, wide_lens, slabs[0], near,
    )
    arrived, near_packed = lax.optimization_barrier((arrived, near_packed))
    relayed = shifted(arrived, "dp", -1)
    pair = (arrived, swapped(arrived, 1))
    best = call(
        functools.partial(early_kernel, chunks=chunks), "early", best_shape, [tops(2)],
        info, starts, counts, near_packed, *pair,
    )
    far_packed, best = call(
        middle_kernel, "middle", (jax.ShapeDtypeStruct((list_rows + spare, width), bf16), best_shape), scratch(1) + [tops(1)],
        info, starts, counts, wide_lens, far, *pair, best,
    )
    relayed, best = lax.optimization_barrier((relayed, best))
    packed, sums = call(
        last_slab_kernel,
        "last_slab",
        (jax.ShapeDtypeStruct((4 * list_rows + spare, width), bf16), jax.ShapeDtypeStruct((mine, LANES), f32)),
        [best_scratch] + scratch(1) + [tops(4)],
        info, starts, counts, wide_lens, far_other, near_packed, far_packed, *pair, best,
    )
    scores = call(
        functools.partial(late_kernel, chunks=chunks), "late", jax.ShapeDtypeStruct((mine, LANES), f32),
        [best_scratch, tops(4)],
        info, starts, counts, packed, relayed, swapped(relayed, 1), sums,
    )

    chip = in_order(scores, swapped(scores, 1), core == 0)
    sent = jnp.where(core == 0, chip[:, :qcount], chip[:, qcount:])
    block = in_order(returned(sent, 0), returned(sent, 2), tok < 2)
    both = in_order(block[None], swapped(block, 1)[None], core == 0)
    return jnp.transpose(both, (2, 0, 1))


def solution(mesh):
    in_specs = (P("dp", None, None), P("dp", "tok", None), P())
    out_specs = P("dp", None, None)
    return jax.shard_map(per_device, mesh=mesh, in_specs=in_specs, out_specs=out_specs, check_vma=False)
```

time: 189 us -> 62.8 us (0.33)
  waiting for transfers between devices: 108 us -> 12.5 us
  matrix products: 31.6 us -> 0 us
  other arithmetic: 28.2 us -> 0.73 us
  starting transfers between devices: 2.47 us -> 26 us
  Pallas kernels: 0 us -> 18.3 us
  between operations: 13.4 us -> 0.11 us
    pmax x1 -> x0, waiting for transfers between devices: 59.8 us -> none  [combine(): merged = lax.pmax(maxima, 'tok')]
    ppermute x2 -> x11, waiting for transfers between devices: 48 us -> 12.5 us  [the longest x2 9.37 us: returned(): return lax.ppermute(block, ('dp', 'tok'), route)]
    dot_general x18 -> x0, matrix products: 31.6 us -> none  [one_group(): lax.dot_general(flat_q, doc_tile, (((1,), (1,)), ((), ())), preferred_ele...]
    ppermute x2 -> x11, starting transfers between devices: 2.47 us -> 26 us  [the longest x7 13.4 us: swapped(): lax.ppermute(block, 'tok', [(i, i ^ mask) for i in range(lax.axis_size('t...]
    pallas_call x0 -> x6, Pallas kernels: none -> 18.3 us  [the longest x5 17.7 us: call(): pl.pallas_call(kernel, out_shape=out_shape, in_specs=[SMEM] * scalar_coun...]
    reduce_max x18 -> x0, other arithmetic: 11.4 us -> none  [one_group(): return (jnp.maximum(running, jnp.max(similar, axis=1)), None)]
    max x18 -> x0, other arithmetic: 6.16 us -> none  [one_group(): return (jnp.maximum(running, jnp.max(similar, axis=1)), None)]
    reduce_sum x4 -> x2, other arithmetic: 5.38 us -> 0.23 us  [the longest x1 0.14 us: per_device(): jnp.sum(jnp.where(index[None, None, :] < index[None, :, None], counts[:,...]
  transfers between devices with their start and end apart: 3 -> 11, of which waited for: 3 -> 5; matrix products, arithmetic and copies ran while one was open for 15% -> 6% of each run, Pallas kernels for 0% -> 20%
where the time goes in v2:
time: 62.8 us
  starting transfers between devices  26 us (41%)
  Pallas kernels  18.3 us (29%)
  waiting for transfers between devices  12.5 us (20%)
  local copies, waits for them, and re-layouts  5.11 us (8%)
  other arithmetic  0.73 us (1%)
    pallas_call x5, Pallas kernels, call(): pl.pallas_call(kernel, out_shape=out_shape, in_specs=[SMEM] * scalar_coun...  17.7 us
    ppermute x7, starting transfers between devices, swapped(): lax.ppermute(block, 'tok', [(i, i ^ mask) for i in range(lax.axis_size('t...  13.4 us
    ppermute x2, starting transfers between devices, shifted(): lax.ppermute(block, axis, [(i, (i + distance) % size) for i in range(size)])  11.6 us
    ppermute x2, waiting for transfers between devices, returned(): return lax.ppermute(block, ('dp', 'tok'), route)  9.37 us
    ppermute x7, waiting for transfers between devices, swapped(): lax.ppermute(block, 'tok', [(i, i ^ mask) for i in range(lax.axis_size('t...  3.12 us
    dynamic_slice x1, local copies, waits for them, and re-layouts, per_device(): lax.dynamic_slice_in_dim(by_slot, (tok ^ k) * mine, mine, 1)  2.33 us
  transfers between devices with their start and end apart: 11, of which 5 were waited for; matrix products, arithmetic and copies ran while one was open for 6% of the time, Pallas kernels for 20%

profile of v2, /device:TPU:1, one launch (start us, length us, event | category | flops | bytes accessed | tf_op | source)
XLA Modules:
  0.0 62.8 jit_solution(6947098824610073238)
XLA Ops:
  0.0 0.0 copy-start
  0.0 1.0 %copy-done = bf16[64,32,128]{2,1,0:T(8,128)(2,1)S(1)} copy-done((bf16[64,32,128]{2,1,0:T(8,128)(2,1)S(1)}, bf16[64,32,128]{2,1,0:T(8,128)(2,1)}, u32[]{:S(2)}) %copy-start) | copy-done | bytes 524312
  1.1 0.6 prepare.1
  1.7 9.7 %collective-permute-start.1 = (bf16[32,32,128]{2,1,0:T(8,128)(2,1)S(1)}, bf16[32,32,128]{2,1,0:T(8,128)(2,1)S(1)}, u32[]{:S(2)}, u32[]{:S(2)}) collective-permute-start(bf16[32,32,128]{2,1,0:T(8,128)(2,1)S(1)} %prepare.1), channel_id=1, source_target_pairs={{0,252},{4,0},{8,4},{12,8},{16,12},{20,16},{24,20},{28,24},{32,28}... | collective-permute-start | bytes 786440 | tf_op jit(solution)/shard_map/ppermute | solution.py:212
  11.4 2.3 %dynamic-slice_bitcast_fusion = (bf16[45,32,128]{2,1,0:T(8,128)(2,1)}, bf16[45,32,128]{2,1,0:T(8,128)(2,1)S(1)}, bf16[45,32,128]{2,1,0:T(8,128)(2,1)S(1)}, bf16[45,32,128]{2,1,0:T(8,128)(2,1)S(1)}) fusion(bf16[128,45,128]{2,0,1:T(8,128)(2,1)} %param.4, s32[]{:T(128)S(6)} %select_n.112, s32[]{:T(128)S(6)} %select_n.110, s32[]{:T(128)S(6)} %select_n.108, ...), kind=kLoop, calls=%fused_computation | loop fusion | bytes 2949136 | tf_op jit(solution)/shard_map/dynamic_slice | solution.py:250
  13.7 2.6 %collective-permute-start.3 = (bf16[45,32,128]{2,1,0:T(8,128)(2,1)}, bf16[45,32,128]{2,1,0:T(8,128)(2,1)S(1)}, u32[]{:S(2)}, u32[]{:S(2)}) collective-permute-start(bf16[45,32,128]{2,1,0:T(8,128)(2,1)} %get-tuple-element.21), channel_id=1, source_target_pairs={{0,2},{1,3},{2,0},{3,1},{4,6},{5,7},{6,4},{7,5},{8,10},{9,11},{10,... | collective-permute-start | bytes 1105928 | tf_op jit(solution)/shard_map/ppermute | solution.py:216
  16.3 1.2 %collective-permute-start.2 = (bf16[45,32,128]{2,1,0:T(8,128)(2,1)S(1)}, bf16[45,32,128]{2,1,0:T(8,128)(2,1)S(1)}, u32[]{:S(2)}, u32[]{:S(2)}) collective-permute-start(bf16[45,32,128]{2,1,0:T(8,128)(2,1)S(1)} %get-tuple-element.24), channel_id=1, source_target_pairs={{0,1},{1,0},{2,3},{3,2},{4,5},{5,4},{6,7},{7,6},{8,9},{9,8},{10,11... | collective-permute-start | bytes 1105928 | tf_op jit(solution)/shard_map/ppermute | solution.py:216
  17.6 0.8 %dynamic_slice.18 = s32[32]{0:T(128)S(1)} dynamic-slice(s32[8192]{0:T(1024)} %param.5, s32[]{:T(128)S(6)} %select_n.102), dynamic_slice_sizes={32} | dynamic-slice | bytes 260 | tf_op jit(solution)/shard_map/dynamic_slice | solution.py:266
  18.3 0.2 subtract_add_fusion
  18.6 0.1 select_reduce_fusion.1
  18.6 0.1 select_reduce_fusion
  18.8 0.1 broadcast_add_fusion
  18.9 0.1 add.79.starts
  18.9 0.1 pad_add_fusion.info
  19.0 0.0 collective-permute-done.2.near
  19.0 0.1 broadcast_in_dim.60.lens
  19.1 3.1 %pack_near.1.packed.near_packed = bf16[3584,128]{1,0:T(8,128)(2,1)S(1)} custom-call(s32[6]{0:T(128)S(1)} %pad_add_fusion.info, s32[128]{0:T(128)S(1)} %add.79.starts, s32[32,128]{1,0:T(8,128)S(1)} %broadcast_in_dim.60.lens, bf16[45,32,128]{2,1,0:T(8,128)(2,1)S(1)} %get-tuple-element.22.own, bf16[45,32,128]{2,1,0:T(8,128)(2,1)S(1)} %collective-permute-done.2.near), custom_call_target="tpu_custom_call" | custom-call | flops 1024 | bytes 1024 | tf_op jit(solution)/shard_map/pack_near/pallas_call | solution.py:293
  22.2 0.0 collective-permute-done.1.qa
  22.2 0.3 collective-permute-start.4
  22.5 1.9 %collective-permute-start.5 = (bf16[32,32,128]{2,1,0:T(8,128)(2,1)S(1)}, bf16[32,32,128]{2,1,0:T(8,128)(2,1)S(1)}, u32[]{:S(2)}, u32[]{:S(2)}) collective-permute-start(bf16[32,32,128]{2,1,0:T(8,128)(2,1)S(1)} %collective-permute-done.1.qa), channel_id=1, source_target_pairs={{0,252},{4,0},{8,4},{12,8},{16,12},{20,16},{24,20},{28,24},{32,28}... | collective-permute-start | bytes 786440 | tf_op jit(solution)/shard_map/ppermute | solution.py:212
  24.4 2.8 %collective-permute-start = (bf16[45,32,128]{2,1,0:T(8,128)(2,1)S(1)}, bf16[45,32,128]{2,1,0:T(8,128)(2,1)S(1)}, u32[]{:S(2)}, u32[]{:S(2)}) collective-permute-start(bf16[45,32,128]{2,1,0:T(8,128)(2,1)S(1)} %get-tuple-element.23), channel_id=1, source_target_pairs={{0,3},{1,2},{2,1},{3,0},{4,7},{5,6},{6,5},{7,4},{8,11},{9,10},{10,... | collective-permute-start | bytes 1105928 | tf_op jit(solution)/shard_map/ppermute | solution.py:216
  27.2 0.1 sub.55
  27.3 0.0 collective-permute-done.4.qb
  27.3 3.7 %early.1.old = f32[512,128]{1,0:T(8,128)S(1)} custom-call(s32[6]{0:T(128)S(1)} %pad_add_fusion.info, s32[128]{0:T(128)S(1)} %add.79.starts, s32[128]{0:T(128)S(1)} %fusion.4.counts, bf16[3584,128]{1,0:T(8,128)(2,1)S(1)} %pack_near.1.packed.near_packed, bf16[32,32,128]{2,1,0:T(8,128)(2,1)S(1)} %collective-permute-done.1.qa, ...), custom_call_target="tpu_custom_call" | custom-call | flops 1024 | bytes 1024 | tf_op jit(solution)/shard_map/early/pallas_call | solution.py:293
  31.0 0.0 collective-permute-done.3.far
  31.0 2.6 %middle.1 = (bf16[2048,128]{1,0:T(8,128)(2,1)S(1)}, f32[512,128]{1,0:T(8,128)S(1)}) custom-call(s32[6]{0:T(128)S(1)} %pad_add_fusion.info, s32[128]{0:T(128)S(1)} %add.79.starts, s32[128]{0:T(128)S(1)} %fusion.4.counts, s32[32,128]{1,0:T(8,128)S(1)} %broadcast_in_dim.60.lens, bf16[45,32,128]{2,1,0:T(8,128)(2,1)S(1)} %collective-permute-done.3.far, ...), custom_call_target="tpu_custom_call" | custom-call | flops 1024 | bytes 1024 | tf_op jit(solution)/shard_map/middle/pallas_call | solution.py:293
  33.7 0.0 collective-permute-done.5.qa
  33.7 1.3 %collective-permute-start.6 = (bf16[32,32,128]{2,1,0:T(8,128)(2,1)S(1)}, bf16[32,32,128]{2,1,0:T(8,128)(2,1)S(1)}, u32[]{:S(2)}, u32[]{:S(2)}) collective-permute-start(bf16[32,32,128]{2,1,0:T(8,128)(2,1)S(1)} %collective-permute-done.5.qa), channel_id=1, source_target_pairs={{0,1},{1,0},{2,3},{3,2},{4,5},{5,4},{6,7},{7,6},{8,9},{9,8},{10,11... | collective-permute-start | bytes 786440 | tf_op jit(solution)/shard_map/ppermute | solution.py:216
  35.0 1.4 %collective-permute-done.far = bf16[45,32,128]{2,1,0:T(8,128)(2,1)S(1)} collective-permute-done((bf16[45,32,128]{2,1,0:T(8,128)(2,1)S(1)}, bf16[45,32,128]{2,1,0:T(8,128)(2,1)S(1)}, u32[]{:S(2)}, u32[]{:S(2)}) %collective-permute-start) | collective-permute-done | bytes 368672 | tf_op jit(solution)/shard_map/ppermute | solution.py:216
  36.4 3.0 %last_slab.1 = (bf16[6656,128]{1,0:T(8,128)(2,1)S(1)}, f32[32,128]{1,0:T(8,128)S(1)}) custom-call(s32[6]{0:T(128)S(1)} %pad_add_fusion.info, s32[128]{0:T(128)S(1)} %add.79.starts, s32[128]{0:T(128)S(1)} %fusion.4.counts, s32[32,128]{1,0:T(8,128)S(1)} %broadcast_in_dim.60.lens, bf16[45,32,128]{2,1,0:T(8,128)(2,1)S(1)} %collective-permute-done.far, ...), custom_call_target="tpu_custom_call" | custom-call | flops 1024 | bytes 1024 | tf_op jit(solution)/shard_map/last_slab/pallas_call | solution.py:293
  39.4 0.0 collective-permute-done.6.qb
  39.4 5.3 %late.1 = f32[32,128]{1,0:T(8,128)S(1)} custom-call(s32[6]{0:T(128)S(1)} %pad_add_fusion.info, s32[128]{0:T(128)S(1)} %add.79.starts, s32[128]{0:T(128)S(1)} %fusion.4.counts, bf16[6656,128]{1,0:T(8,128)(2,1)S(1)} %get-tuple-element.18.packed, bf16[32,32,128]{2,1,0:T(8,128)(2,1)S(1)} %collective-permute-done.5.qa, ...), custom_call_target="tpu_custom_call" | custom-call | flops 1024 | bytes 1024 | tf_op jit(solution)/shard_map/late/pallas_call | solution.py:293
  44.7 0.4 collective-permute-start.7
  45.1 0.8 %collective-permute-done.7 = f32[32,128]{1,0:T(8,128)S(1)} collective-permute-done((f32[32,128]{1,0:T(8,128)S(1)}, f32[32,128]{1,0:T(8,128)S(1)}, u32[]{:S(2)}, u32[]{:S(2)}) %collective-permute-start.7) | collective-permute-done | bytes 16416 | tf_op jit(solution)/shard_map/ppermute | solution.py:216
  46.0 0.1 slice_select_fusion
  46.1 0.0 collective-permute-start.9
  46.1 1.0 %collective-permute-start.8 = (f32[64,64]{1,0:T(8,128)S(1)}, f32[64,64]{1,0:T(8,128)S(1)}, u32[]{:S(2)}, u32[]{:S(2)}) collective-permute-start(f32[64,64]{1,0:T(8,128)S(1)} %slice_select_fusion), channel_id=1, source_target_pairs={{0,4},{1,9},{2,6},{3,11},{4,8},{5,13},{6,10},{7,15},{8,12},{9,17},... | collective-permute-start | bytes 49160 | tf_op jit(solution)/shard_map/ppermute | solution.py:226
  47.1 8.1 %collective-permute-done.9 = f32[64,64]{1,0:T(8,128)S(1)} collective-permute-done((f32[64,64]{1,0:T(8,128)S(1)}, f32[64,64]{1,0:T(8,128)S(1)}, u32[]{:S(2)}, u32[]{:S(2)}) %collective-permute-start.9) | collective-permute-done | bytes 16416 | tf_op jit(solution)/shard_map/ppermute | solution.py:226
  55.2 1.3 %collective-permute-done.8 = f32[64,64]{1,0:T(8,128)S(1)} collective-permute-done((f32[64,64]{1,0:T(8,128)S(1)}, f32[64,64]{1,0:T(8,128)S(1)}, u32[]{:S(2)}, u32[]{:S(2)}) %collective-permute-start.8) | collective-permute-done | bytes 16416 | tf_op jit(solution)/shard_map/ppermute | solution.py:226
  56.4 4.7 %collective-permute-start.10 = (f32[128,64]{1,0:T(8,128)S(1)}, f32[128,64]{1,0:T(8,128)S(1)}, u32[]{:S(2)}, u32[]{:S(2)}) collective-permute-start(f32[128,64]{1,0:T(8,128)S(1)} %maximum_select_fusion.2), channel_id=1, source_target_pairs={{0,1},{1,0},{2,3},{3,2},{4,5},{5,4},{6,7},{7,6},{8,9},{9,8},{10,11... | collective-permute-start | bytes 98312 | tf_op jit(solution)/shard_map/ppermute | solution.py:216
  61.2 0.9 %collective-permute-done.10 = f32[128,64]{1,0:T(8,128)S(1)} collective-permute-done((f32[128,64]{1,0:T(8,128)S(1)}, f32[128,64]{1,0:T(8,128)S(1)}, u32[]{:S(2)}, u32[]{:S(2)}) %collective-permute-start.10) | collective-permute-done | bytes 32800 | tf_op jit(solution)/shard_map/ppermute | solution.py:216
  62.1 0.7 %copy.5 = f32[64,2,128]{2,1,0:T(2,128)} copy(f32[64,2,128]{0,2,1:T(8,128)S(1)} %fusion) | data formatting | bytes 131072 | tf_op jit(solution)/shard_map/transpose | solution.py:337
  (11 shorter events, 0.1 us)
Async XLA Ops:
  0.0 1.0 %copy-start = (bf16[64,32,128]{2,1,0:T(8,128)(2,1)S(1)}, bf16[64,32,128]{2,1,0:T(8,128)(2,1)}, u32[]{:S(2)}) copy-start(bf16[64,32,128]{2,1,0:T(8,128)(2,1)} %param.3) | copy-start | bytes 1572868
  1.7 20.5 %collective-permute-start.1 = (bf16[32,32,128]{2,1,0:T(8,128)(2,1)S(1)}, bf16[32,32,128]{2,1,0:T(8,128)(2,1)S(1)}, u32[]{:S(2)}, u32[]{:S(2)}) collective-permute-start(bf16[32,32,128]{2,1,0:T(8,128)(2,1)S(1)} %prepare.1), channel_id=1, source_target_pairs={{0,252},{4,0},{8,4},{12,8},{16,12},{20,16},{24,20},{28,24},{32,28}... | collective-permute-start | bytes 786440 | tf_op jit(solution)/shard_map/ppermute | solution.py:212
  13.7 17.3 %collective-permute-start.3 = (bf16[45,32,128]{2,1,0:T(8,128)(2,1)}, bf16[45,32,128]{2,1,0:T(8,128)(2,1)S(1)}, u32[]{:S(2)}, u32[]{:S(2)}) collective-permute-start(bf16[45,32,128]{2,1,0:T(8,128)(2,1)} %get-tuple-element.21), channel_id=1, source_target_pairs={{0,2},{1,3},{2,0},{3,1},{4,6},{5,7},{6,4},{7,5},{8,10},{9,11},{10,... | collective-permute-start | bytes 1105928 | tf_op jit(solution)/shard_map/ppermute | solution.py:216
  16.3 2.7 %collective-permute-start.2 = (bf16[45,32,128]{2,1,0:T(8,128)(2,1)S(1)}, bf16[45,32,128]{2,1,0:T(8,128)(2,1)S(1)}, u32[]{:S(2)}, u32[]{:S(2)}) collective-permute-start(bf16[45,32,128]{2,1,0:T(8,128)(2,1)S(1)} %get-tuple-element.24), channel_id=1, source_target_pairs={{0,1},{1,0},{2,3},{3,2},{4,5},{5,4},{6,7},{7,6},{8,9},{9,8},{10,11... | collective-permute-start | bytes 1105928 | tf_op jit(solution)/shard_map/ppermute | solution.py:216
  22.2 5.1 %collective-permute-start.4 = (bf16[32,32,128]{2,1,0:T(8,128)(2,1)S(1)}, bf16[32,32,128]{2,1,0:T(8,128)(2,1)S(1)}, u32[]{:S(2)}, u32[]{:S(2)}) collective-permute-start(bf16[32,32,128]{2,1,0:T(8,128)(2,1)S(1)} %collective-permute-done.1.qa), channel_id=1, source_target_pairs={{0,1},{1,0},{2,3},{3,2},{4,5},{5,4},{6,7},{7,6},{8,9},{9,8},{10,11... | collective-permute-start | bytes 786440 | tf_op jit(solution)/shard_map/ppermute | solution.py:216
  22.5 11.2 %collective-permute-start.5 = (bf16[32,32,128]{2,1,0:T(8,128)(2,1)S(1)}, bf16[32,32,128]{2,1,0:T(8,128)(2,1)S(1)}, u32[]{:S(2)}, u32[]{:S(2)}) collective-permute-start(bf16[32,32,128]{2,1,0:T(8,128)(2,1)S(1)} %collective-permute-done.1.qa), channel_id=1, source_target_pairs={{0,252},{4,0},{8,4},{12,8},{16,12},{20,16},{24,20},{28,24},{32,28}... | collective-permute-start | bytes 786440 | tf_op jit(solution)/shard_map/ppermute | solution.py:212
  24.4 12.0 %collective-permute-start = (bf16[45,32,128]{2,1,0:T(8,128)(2,1)S(1)}, bf16[45,32,128]{2,1,0:T(8,128)(2,1)S(1)}, u32[]{:S(2)}, u32[]{:S(2)}) collective-permute-start(bf16[45,32,128]{2,1,0:T(8,128)(2,1)S(1)} %get-tuple-element.23), channel_id=1, source_target_pairs={{0,3},{1,2},{2,1},{3,0},{4,7},{5,6},{6,5},{7,4},{8,11},{9,10},{10,... | collective-permute-start | bytes 1105928 | tf_op jit(solution)/shard_map/ppermute | solution.py:216
  33.7 5.8 %collective-permute-start.6 = (bf16[32,32,128]{2,1,0:T(8,128)(2,1)S(1)}, bf16[32,32,128]{2,1,0:T(8,128)(2,1)S(1)}, u32[]{:S(2)}, u32[]{:S(2)}) collective-permute-start(bf16[32,32,128]{2,1,0:T(8,128)(2,1)S(1)} %collective-permute-done.5.qa), channel_id=1, source_target_pairs={{0,1},{1,0},{2,3},{3,2},{4,5},{5,4},{6,7},{7,6},{8,9},{9,8},{10,11... | collective-permute-start | bytes 786440 | tf_op jit(solution)/shard_map/ppermute | solution.py:216
  44.7 1.3 %collective-permute-start.7 = (f32[32,128]{1,0:T(8,128)S(1)}, f32[32,128]{1,0:T(8,128)S(1)}, u32[]{:S(2)}, u32[]{:S(2)}) collective-permute-start(f32[32,128]{1,0:T(8,128)S(1)} %late.1), channel_id=1, source_target_pairs={{0,1},{1,0},{2,3},{3,2},{4,5},{5,4},{6,7},{7,6},{8,9},{9,8},{10,11... | collective-permute-start | bytes 49160 | tf_op jit(solution)/shard_map/ppermute | solution.py:216
  46.1 9.1 %collective-permute-start.9 = (f32[64,64]{1,0:T(8,128)S(1)}, f32[64,64]{1,0:T(8,128)S(1)}, u32[]{:S(2)}, u32[]{:S(2)}) collective-permute-start(f32[64,64]{1,0:T(8,128)S(1)} %slice_select_fusion), channel_id=1, source_target_pairs={{0,6},{1,11},{2,4},{3,9},{4,10},{5,15},{6,8},{7,13},{8,14},{9,19},... | collective-permute-start | bytes 49160 | tf_op jit(solution)/shard_map/ppermute | solution.py:226
  46.1 10.3 %collective-permute-start.8 = (f32[64,64]{1,0:T(8,128)S(1)}, f32[64,64]{1,0:T(8,128)S(1)}, u32[]{:S(2)}, u32[]{:S(2)}) collective-permute-start(f32[64,64]{1,0:T(8,128)S(1)} %slice_select_fusion), channel_id=1, source_target_pairs={{0,4},{1,9},{2,6},{3,11},{4,8},{5,13},{6,10},{7,15},{8,12},{9,17},... | collective-permute-start | bytes 49160 | tf_op jit(solution)/shard_map/ppermute | solution.py:226
  56.4 5.6 %collective-permute-start.10 = (f32[128,64]{1,0:T(8,128)S(1)}, f32[128,64]{1,0:T(8,128)S(1)}, u32[]{:S(2)}, u32[]{:S(2)}) collective-permute-start(f32[128,64]{1,0:T(8,128)S(1)} %maximum_select_fusion.2), channel_id=1, source_target_pairs={{0,1},{1,0},{2,3},{3,2},{4,5},{5,4},{6,7},{7,6},{8,9},{9,8},{10,11... | collective-permute-start | bytes 98312 | tf_op jit(solution)/shard_map/ppermute | solution.py:216

commit v3 on v0

v3 whole, which is shorter than its diff:
```python
import functools

import jax
import jax.numpy as jnp
from jax import lax
from jax.experimental import pallas as pl
from jax.experimental.pallas import tpu as pltpu
from jax.sharding import PartitionSpec as P

STEPS = 2
NEGATIVE_FILL = -1e30
CHUNK = 16
GROUP = 8
BLOCK = CHUNK * GROUP
BATCH = 8
COLUMNS = 256
LANES = 128
RUN = 8
FAR = (3, 2)
SLABS = (0, 1) + FAR
VMEM_LIMIT = 40 * 1024 * 1024
CUT_VMEM_LIMIT = 62 * 1024 * 1024
SMEM = pl.BlockSpec(memory_space=pltpu.SMEM)
VMEM = pl.BlockSpec(memory_space=pltpu.VMEM)
HBM = pl.BlockSpec(memory_space=pltpu.HBM)


def normalized(values):
    wide = values.astype(jnp.float32)
    return wide * lax.rsqrt(jnp.sum(wide * wide, axis=-1, keepdims=True) + 1e-06)


def prepare_kernel(half_ref, out_ref, wide_ref):
    count, tokens, _ = half_ref.shape

    def norm_one(i, carry):
        rows = pl.ds(pl.multiple_of(i * tokens, tokens), tokens)
        wide_ref[rows, :] = normalized(half_ref[i])
        return carry

    lax.fori_loop(0, count, norm_one, 0, unroll=16)

    def place_token(k, carry):
        out_ref[k] = wide_ref[pl.ds(k, count, stride=tokens), :].astype(out_ref.dtype)
        return carry

    lax.fori_loop(0, tokens, place_token, 0, unroll=16)


def cut_kernel(docs_ref, after_ref, *refs):
    del after_ref
    *slab_refs, sems = refs
    mine = slab_refs[0].shape[1]
    cuts = []
    for n in (2, 3, 1, 0):
        first = pl.multiple_of((lax.axis_index("tok") ^ SLABS[n]) * mine, mine)
        cuts.append(pltpu.make_async_copy(docs_ref.at[:, pl.ds(first, mine), :], slab_refs[n], sems.at[n]))
        cuts[-1].start()
    for cut in cuts:
        cut.wait()


def pack(slab_ref, base, starts, first_entry, offset, sort_ref, tall_ref, packed_ref):
    slots, docs, width = slab_ref.shape
    groups = docs // GROUP
    step = sort_ref.shape[0] // docs
    first = normalized(slab_ref[0])
    firsts = jnp.concatenate([first] * step, axis=0)
    slot = lax.broadcasted_iota(jnp.int32, (step * docs, 1), 0) // docs + base
    for u in range(0, -(-slots // CHUNK) * CHUNK, step):
        inside = min(slots - u, step)
        rows = normalized(slab_ref[u : u + inside]).reshape(inside * docs, width)
        if inside < step:
            rows = jnp.concatenate([rows] + [first] * (step - inside), axis=0)
        rows = jnp.where(slot + u < tall_ref[...], rows, firsts).astype(packed_ref.dtype)
        rows = jnp.dot(sort_ref[...], rows, preferred_element_type=jnp.float32)
        start = (starts[first_entry + u // CHUNK] - offset) * BLOCK
        for g in range(groups):
            for v in range(0, step, 2):
                both = [rows[(v + e) * docs + g * GROUP : (v + e) * docs + (g + 1) * GROUP] for e in range(2)]
                at = pl.multiple_of(start + (g * BLOCK + (u % CHUNK + v) * GROUP), 2 * GROUP)
                packed_ref[pl.ds(at, 2 * GROUP), :] = jnp.concatenate(both, axis=0).astype(packed_ref.dtype)


def multiply(packed_ref, count, q_refs, top_ref, batch_blocks=BATCH):
    tokens, queries, width = q_refs[0].shape
    step = COLUMNS // queries

    def run(s, blocks):
        rows = packed_ref[pl.ds(pl.multiple_of(s * BLOCK, BLOCK), blocks * BLOCK), :]
        at = 0
        for q_ref in q_refs:
            for k in range(0, tokens, step):
                q = q_ref[k : k + step].reshape(COLUMNS, width)
                similar = lax.dot_general(rows, q, (((1,), (1,)), ((), ())), preferred_element_type=jnp.float32)
                top = jnp.max(similar.reshape(blocks, CHUNK, GROUP, COLUMNS), axis=1)
                place = pl.ds(pl.multiple_of(s * GROUP, GROUP), blocks * GROUP)
                top_ref[place, at : at + COLUMNS] = top.reshape(blocks * GROUP, COLUMNS)
                at += COLUMNS

    def batch(i, carry):
        run(i * batch_blocks, batch_blocks)
        return carry

    lax.fori_loop(0, count // batch_blocks, batch, 0)
    size = batch_blocks // 2
    while size:
        done = count // (2 * size) * (2 * size)

        @pl.when(count - done >= size)
        def _(size=size, done=done):
            run(done, size)

        size //= 2


def combine(top_ref, lists, offset, starts, lens_ref, old_ref, best_ref, slots, first=0):
    docs, columns = best_ref.shape
    chunks = (starts.shape[0] - 1) // 4
    for g in range(docs // GROUP):
        rows = slice(g * GROUP, (g + 1) * GROUP)
        lens = lens_ref[rows, 0:1]
        best = jnp.full((GROUP, columns), NEGATIVE_FILL, jnp.float32) if old_ref is None else old_ref[rows, :]
        for which in lists:
            for c in range(chunks):
                at = pl.multiple_of((starts[which * chunks + c] - offset + g) * GROUP, GROUP)
                top = top_ref[pl.ds(at, GROUP), first : first + columns]
                real = lens > (lax.axis_index("tok") ^ SLABS[which]) * slots + c * CHUNK
                best = jnp.maximum(best, jnp.where(real, top, NEGATIVE_FILL))
        best_ref[rows, :] = best


def pack_kernel(starts, sort, tall, own, near, packed_ref, *, slots, chunks):
    tok = lax.axis_index("tok")
    for k, slab in enumerate((own, near)):
        pack(slab, (tok ^ k) * slots, starts, k * chunks, 0, sort, tall, packed_ref)


def early_kernel(starts, lens, packed, qa, qb, best_ref, top_ref, *, slots, chunks):
    multiply(packed, starts[2 * chunks], (qa, qb), top_ref)
    combine(top_ref, (0, 1), 0, starts, lens, None, best_ref, slots)


def middle_kernel(starts, lens, sort, tall, far, qa, qb, old, packed_ref, best_ref, top_ref, *, slots, chunks):
    offset = starts[2 * chunks]
    pack(far, (lax.axis_index("tok") ^ FAR[0]) * slots, starts, 2 * chunks, offset, sort, tall, packed_ref)
    multiply(packed_ref, starts[3 * chunks] - offset, (qa, qb), top_ref)
    combine(top_ref, (2,), offset, starts, lens, old, best_ref, slots)


def second_kernel(starts, lens, near_packed, far_packed, qa, qb, best_ref, near_top, far_top, *, slots, chunks):
    offset = starts[2 * chunks]
    multiply(near_packed, offset, (qa, qb), near_top)
    multiply(far_packed, starts[3 * chunks] - offset, (qa, qb), far_top)
    combine(near_top, (0, 1), 0, starts, lens, None, best_ref, slots)
    combine(far_top, (2,), offset, starts, lens, best_ref, best_ref, slots)


def query_sums(best_ref, step_no, tok, count):
    docs, columns = best_ref.shape
    half = lax.rem(tok, 2)
    lane_group = lax.broadcasted_iota(jnp.int32, (docs, LANES), 1) // count
    merged = jnp.zeros((docs, LANES), jnp.float32)
    for other in range(2):
        at = other * columns // 2
        total = best_ref[:, at : at + LANES]
        for k in range(at + LANES, at + columns // 2, LANES):
            total = total + best_ref[:, k : k + LANES]
        shift = LANES // 2
        while shift >= count:
            total = total + pltpu.roll(total, shift, 1)
            shift //= 2
        place = 2 * step_no + (half if other == 0 else 1 - half)
        merged = jnp.where(lane_group == place, total, merged)
    return merged


def late_kernel(
    starts, order, lens, sort, tall, far, q1a, q1b, q2a, q2b, old1, old2, out_ref,
    best_ref, packed_ref, top_ref, sums_ref, *, slots, chunks,
):
    tok = lax.axis_index("tok")
    offset = starts[3 * chunks]
    pack(far, (tok ^ FAR[1]) * slots, starts, 3 * chunks, offset, sort, tall, packed_ref)
    multiply(packed_ref, starts[4 * chunks] - offset, (q1a, q1b, q2a, q2b), top_ref, BATCH // 2)
    docs, columns = best_ref.shape
    total = jnp.zeros((docs, LANES), jnp.float32)
    for s, old in enumerate((old1, old2)):
        combine(top_ref, (3,), offset, starts, lens, old, best_ref, slots, s * columns)
        total = total + query_sums(best_ref, s, tok, q1a.shape[1])
    sums_ref[...] = total

    def unsort(p, carry):
        out_ref[pl.ds(order[p], 1), :] = sums_ref[pl.ds(p, 1), :]
        return carry

    lax.fori_loop(0, docs, unsort, 0, unroll=8)


def wraps(dp, shift):
    return dp % RUN < shift


def handed_back(block, shift, chosen=lambda dp: True):
    dp_size, tok_size = lax.axis_size("dp"), lax.axis_size("tok")
    route = []
    for i in filter(chosen, range(dp_size)):
        for t in range(tok_size):
            mask = 2 if t % 2 and i % (dp_size // 2) < shift else 0
            route.append((i * tok_size + t, (i - shift) % dp_size * tok_size + (t ^ mask)))
    return lax.ppermute(block, ("dp", "tok"), route)


def swapped(block, mask):
    return lax.ppermute(block, "tok", [(i, i ^ mask) for i in range(lax.axis_size("tok"))])


def returned(block, mask):
    dp_size, tok_size = lax.axis_size("dp"), lax.axis_size("tok")
    route = [
        (i * tok_size + t, (i + 1 + t % 2) % dp_size * tok_size + (t ^ mask))
        for i in range(dp_size)
        for t in range(tok_size)
    ]
    return lax.ppermute(block, ("dp", "tok"), route)


def in_order(own, other, own_first):
    return jnp.where(own_first, jnp.concatenate([own, other], axis=0), jnp.concatenate([other, own], axis=0))


def per_device(queries, documents, lengths):
    qcount, tokens, width = queries.shape
    dcount, slots, _ = documents.shape
    tok_size = lax.axis_size("tok")
    tok, dp = lax.axis_index("tok"), lax.axis_index("dp")
    core = tok % 2
    mine = dcount // tok_size
    half = qcount // 2
    columns = qcount * tokens
    chunks = -(-slots // CHUNK)
    groups = mine // GROUP
    params = pltpu.CompilerParams(vmem_limit_bytes=VMEM_LIMIT)
    cost = pl.CostEstimate(flops=1 << 10, bytes_accessed=1 << 10, transcendentals=0)
    bf16, f32 = jnp.bfloat16, jnp.float32

    def call(kernel, name, out_shape, scratch_shapes, scalars, *operands):
        return pl.pallas_call(
            kernel,
            out_shape=out_shape,
            in_specs=[SMEM] * len(scalars) + [VMEM] * len(operands),
            out_specs=jax.tree.map(lambda _: VMEM, out_shape),
            scratch_shapes=scratch_shapes,
            compiler_params=params,
            cost_estimate=cost,
            name=name,
        )(*scalars, *operands)

    prepared = call(
        prepare_kernel, "prepare", jax.ShapeDtypeStruct((tokens, half, width), bf16),
        [pltpu.VMEM((half * tokens, width), f32)], (), lax.dynamic_slice_in_dim(queries, core * half, half, 0),
    )
    arrived = handed_back(prepared, 1)
    slabs = pl.pallas_call(
        cut_kernel,
        out_shape=(jax.ShapeDtypeStruct((slots, mine, width), bf16),) * tok_size,
        in_specs=[HBM, HBM],
        out_specs=(VMEM,) * tok_size,
        scratch_shapes=[pltpu.SemaphoreType.DMA((tok_size,))],
        compiler_params=pltpu.CompilerParams(vmem_limit_bytes=CUT_VMEM_LIMIT),
        cost_estimate=cost,
        name="cut",
    )(jnp.transpose(documents, (1, 0, 2)), prepared)
    own, prepared = lax.optimization_barrier((slabs[0], prepared))
    relayed = handed_back(arrived, 1, lambda i: not wraps(i + 1, 2)) + handed_back(prepared, 2, lambda i: wraps(i, 2))
    near, *fars = [swapped(slabs[n], SLABS[n]) for n in (1, 2, 3)]

    lens = lax.dynamic_slice_in_dim(lengths, dp * dcount + tok * mine, mine, 0)
    index = jnp.arange(mine, dtype=jnp.int32)
    ahead = (lens[None, :] > lens[:, None]) | ((lens[None, :] == lens[:, None]) & (index[None, :] < index[:, None]))
    rank = jnp.sum(ahead.astype(jnp.int32), axis=1)
    at = rank[None, :] == index[:, None]
    order = jnp.sum(jnp.where(at, index[None, :], 0), axis=1)
    sorted_lens = jnp.sum(jnp.where(at, lens[None, :], 0), axis=1)
    wide_lens = jnp.broadcast_to(sorted_lens[:, None], (mine, LANES))
    row = jnp.arange(LANES)
    same = row[:, None] // mine == row[None, :] // mine
    sort = (same & (jnp.tile(rank, LANES // mine)[None, :] == row[:, None] % mine)).astype(bf16)
    tall = jnp.broadcast_to(jnp.tile(lens, LANES // mine)[:, None], (LANES, LANES))
    slab, chunk = jnp.array(SLABS)[:, None], jnp.arange(chunks)[None, :]
    least = ((tok ^ slab) * slots + chunk * CHUNK).reshape(-1)
    used = jnp.sum((sorted_lens[::GROUP][None, :] > least[:, None]).astype(jnp.int32), axis=1)
    entry = jnp.arange(tok_size * chunks + 1)
    starts = jnp.sum(jnp.where(entry[None, :-1] < entry[:, None], used[None, :], 0), axis=1)

    def packed_shape(lists):
        return jax.ShapeDtypeStruct(((lists * chunks + 1) * groups * BLOCK, width), bf16)

    def tops(lists, steps=1):
        return pltpu.VMEM(((lists * chunks + 1) * groups * GROUP, steps * columns), f32)

    shapes = dict(slots=slots, chunks=chunks)
    best_shape = jax.ShapeDtypeStruct((mine, columns), f32)
    near_packed = call(
        functools.partial(pack_kernel, **shapes), "pack_near", packed_shape(2), [], (starts,), sort, tall, own, near,
    )
    pair = (arrived, swapped(arrived, 1))
    best = call(
        functools.partial(early_kernel, **shapes), "early", best_shape, [tops(2)], (starts,),
        wide_lens, near_packed, *pair,
    )
    relayed, best = lax.optimization_barrier((relayed, best))
    last_pair = (relayed, swapped(relayed, 1))
    far_packed, best = call(
        functools.partial(middle_kernel, **shapes), "middle", (packed_shape(1), best_shape), [tops(1)], (starts,),
        wide_lens, sort, tall, fars[0], *pair, best,
    )
    second = call(
        functools.partial(second_kernel, **shapes), "second", best_shape, [tops(2), tops(1)], (starts,),
        wide_lens, near_packed, far_packed, *last_pair,
    )
    scores = call(
        functools.partial(late_kernel, **shapes), "late", jax.ShapeDtypeStruct((mine, LANES), f32),
        [
            pltpu.VMEM((mine, columns), f32),
            pltpu.VMEM(packed_shape(1).shape, bf16),
            tops(1, STEPS),
            pltpu.VMEM((mine, LANES), f32),
        ],
        (starts, order), wide_lens, sort, tall, fars[1], *pair, *last_pair, best, second,
    )

    chip = in_order(scores, swapped(scores, 1), core == 0)
    sent = jnp.where(core == 0, chip[:, :qcount], chip[:, qcount:])
    block = in_order(returned(sent, 0), returned(sent, 2), tok < 2)
    both = in_order(block[None], swapped(block, 1)[None], core == 0)
    return jnp.transpose(both, (2, 0, 1))


def solution(mesh):
    in_specs = (P("dp", None, None), P("dp", "tok", None), P())
    out_specs = P("dp", None, None)
    return jax.shard_map(per_device, mesh=mesh, in_specs=in_specs, out_specs=out_specs, check_vma=False)
```

time: 189 us -> 60.5 us (0.32)
  waiting for transfers between devices: 108 us -> 9.17 us
  matrix products: 31.6 us -> 0 us
  other arithmetic: 28.2 us -> 0.87 us
  starting transfers between devices: 2.47 us -> 26.4 us
  Pallas kernels: 0 us -> 19.8 us
  between operations: 13.4 us -> 0.24 us
    pmax x1 -> x0, waiting for transfers between devices: 59.8 us -> none  [combine(): merged = lax.pmax(maxima, 'tok')]
    ppermute x2 -> x12, waiting for transfers between devices: 48 us -> 9.17 us  [the longest x2 7.1 us: returned(): return lax.ppermute(block, ('dp', 'tok'), route)]
    dot_general x18 -> x0, matrix products: 31.6 us -> none  [one_group(): lax.dot_general(flat_q, doc_tile, (((1,), (1,)), ((), ())), preferred_ele...]
    ppermute x2 -> x12, starting transfers between devices: 2.47 us -> 26.4 us  [the longest x3 16.4 us: handed_back(): return lax.ppermute(block, ('dp', 'tok'), route)]
    pallas_call x0 -> x7, Pallas kernels: none -> 19.8 us  [the longest x6 17.3 us: call(): pl.pallas_call(kernel, out_shape=out_shape, in_specs=[SMEM] * len(scalars...]
    reduce_max x18 -> x0, other arithmetic: 11.4 us -> none  [one_group(): return (jnp.maximum(running, jnp.max(similar, axis=1)), None)]
    max x18 -> x0, other arithmetic: 6.16 us -> none  [one_group(): return (jnp.maximum(running, jnp.max(similar, axis=1)), None)]
    reduce_sum x4, other arithmetic: 5.38 us -> 0.5 us  [the longest x1 0.18 us: per_device(): rank = jnp.sum(ahead.astype(jnp.int32), axis=1)]
  transfers between devices with their start and end apart: 3 -> 12, of which waited for: 3 -> 4; matrix products, arithmetic and copies ran while one was open for 15% -> 3% of each run, Pallas kernels for 0% -> 27%
where the time goes in v3:
time: 60.5 us
  starting transfers between devices  26.4 us (44%)
  Pallas kernels  19.8 us (33%)
  waiting for transfers between devices  9.17 us (15%)
  local copies, waits for them, and re-layouts  4.03 us (7%)
  other arithmetic  0.87 us (1%)
    pallas_call x6, Pallas kernels, call(): pl.pallas_call(kernel, out_shape=out_shape, in_specs=[SMEM] * len(scalars...  17.3 us
    ppermute x3, starting transfers between devices, handed_back(): return lax.ppermute(block, ('dp', 'tok'), route)  16.4 us
    ppermute x2, waiting for transfers between devices, returned(): return lax.ppermute(block, ('dp', 'tok'), route)  7.1 us
    ppermute x7, starting transfers between devices, swapped(): lax.ppermute(block, 'tok', [(i, i ^ mask) for i in range(lax.axis_size('t...  5.97 us
    ppermute x2, starting transfers between devices, returned(): return lax.ppermute(block, ('dp', 'tok'), route)  4.03 us
    pallas_call x1, Pallas kernels, per_device(): pl.pallas_call(cut_kernel, out_shape=(jax.ShapeDtypeStruct((slots, mine,...  2.52 us
    ppermute x7, waiting for transfers between devices, swapped(): lax.ppermute(block, 'tok', [(i, i ^ mask) for i in range(lax.axis_size('t...  2.07 us
    unnamed x8, local copies, waits for them, and re-layouts  2.04 us
  transfers between devices with their start and end apart: 12, of which 4 were waited for; matrix products, arithmetic and copies ran while one was open for 3% of the time, Pallas kernels for 27%

profile of v3, /device:TPU:1, one launch (start us, length us, event | category | flops | bytes accessed | tf_op | source)
XLA Modules:
  0.0 60.5 jit_solution(11803097459919611525)
XLA Ops:
  0.0 0.0 copy-start
  0.0 0.0 copy-start.3
  0.0 1.0 %copy-done = bf16[64,32,128]{2,1,0:T(8,128)(2,1)S(1)} copy-done((bf16[64,32,128]{2,1,0:T(8,128)(2,1)S(1)}, bf16[64,32,128]{2,1,0:T(8,128)(2,1)}, u32[]{:S(2)}) %copy-start) | copy-done | bytes 524312
  1.1 0.6 prepare.1.after_ref
  1.7 0.0 copy-start.1
  1.7 11.1 %collective-permute-start.1 = (bf16[32,32,128]{2,1,0:T(8,128)(2,1)S(1)}, bf16[32,32,128]{2,1,0:T(8,128)(2,1)S(1)}, u32[]{:S(2)}, u32[]{:S(2)}) collective-permute-start(bf16[32,32,128]{2,1,0:T(8,128)(2,1)S(1)} %prepare.1.after_ref), channel_id=1, source_target_pairs={{0,252},{1,255},{2,254},{3,253},{4,0},{5,1},{6,2},{7,3},{8,4},{9,5... | collective-permute-start | bytes 786440 | tf_op jit(solution)/shard_map/ppermute | solution.py:211
  12.8 0.0 copy-done.1
  12.8 2.5 %cut.1 = (bf16[45,32,128]{2,1,0:T(8,128)(2,1)}, bf16[45,32,128]{2,1,0:T(8,128)(2,1)}, bf16[45,32,128]{2,1,0:T(8,128)(2,1)}, bf16[45,32,128]{2,1,0:T(8,128)(2,1)}) custom-call(bf16[45,128,128]{2,1,0:T(8,128)(2,1)} %bitcast.7, bf16[32,32,128]{2,1,0:T(8,128)(2,1)} %copy-done.1), custom_call_target="tpu_custom_call" | custom-call | flops 1024 | bytes 1024 | tf_op jit(solution)/shard_map/cut/pallas_call | solution.py:264
  15.3 0.1 collective-permute-start.5
  15.4 4.0 %collective-permute-start.4 = (bf16[32,32,128]{2,1,0:T(8,128)(2,1)}, bf16[32,32,128]{2,1,0:T(8,128)(2,1)S(1)}, u32[]{:S(2)}, u32[]{:S(2)}) collective-permute-start(bf16[32,32,128]{2,1,0:T(8,128)(2,1)} %copy-done.1), channel_id=1, source_target_pairs={{0,248},{1,251},{2,250},{3,249},{4,252},{5,255},{6,254},{7,253},{3... | collective-permute-start | bytes 786440 | tf_op jit(solution)/shard_map/ppermute | solution.py:211
  19.5 1.5 %collective-permute-start.7 = (bf16[45,32,128]{2,1,0:T(8,128)(2,1)}, bf16[45,32,128]{2,1,0:T(8,128)(2,1)S(1)}, u32[]{:S(2)}, u32[]{:S(2)}) collective-permute-start(bf16[45,32,128]{2,1,0:T(8,128)(2,1)} %get-tuple-element.21), channel_id=1, source_target_pairs={{0,3},{1,2},{2,1},{3,0},{4,7},{5,6},{6,5},{7,4},{8,11},{9,10},{10,... | collective-permute-start | bytes 1105928 | tf_op jit(solution)/shard_map/ppermute | solution.py:215
  20.9 0.8 %dynamic_slice.6 = s32[32]{0:T(128)S(1)} dynamic-slice(s32[8192]{0:T(1024)} %param.6, s32[]{:T(128)S(6)} %select_n.101), dynamic_slice_sizes={32} | dynamic-slice | bytes 260 | tf_op jit(solution)/shard_map/dynamic_slice | solution.py:278
  21.7 0.2 convert_reduce_fusion
  21.9 0.0 copy-done.3
  21.9 0.1 eq.33
  22.0 0.1 and_convert_fusion.sort
  22.1 0.1 broadcast_add_fusion
  22.2 0.0 collective-permute-done.1.qa.q1a
  22.2 0.0 collective-permute-start.2
  22.2 1.3 %collective-permute-start.3 = (bf16[32,32,128]{2,1,0:T(8,128)(2,1)S(1)}, bf16[32,32,128]{2,1,0:T(8,128)(2,1)S(1)}, u32[]{:S(2)}, u32[]{:S(2)}) collective-permute-start(bf16[32,32,128]{2,1,0:T(8,128)(2,1)S(1)} %collective-permute-done.1.qa.q1a), channel_id=1, source_target_pairs={{4,0},{5,1},{6,2},{7,3},{8,4},{9,5},{10,6},{11,7},{12,8},{13,9},{1... | collective-permute-start | bytes 786440 | tf_op jit(solution)/shard_map/ppermute | solution.py:211
  23.5 0.1 select_reduce_fusion
  23.6 0.1 slice.13
  23.7 0.1 add.65
  23.8 0.1 broadcast_in_dim.34
  23.9 0.1 convert_reduce_fusion.1
  24.0 0.0 collective-permute-done.5.near
  24.0 2.1 %collective-permute-start = (bf16[45,32,128]{2,1,0:T(8,128)(2,1)}, bf16[45,32,128]{2,1,0:T(8,128)(2,1)S(1)}, u32[]{:S(2)}, u32[]{:S(2)}) collective-permute-start(bf16[45,32,128]{2,1,0:T(8,128)(2,1)} %get-tuple-element.15), channel_id=1, source_target_pairs={{0,2},{1,3},{2,0},{3,1},{4,6},{5,7},{6,4},{7,5},{8,10},{9,11},{10,... | collective-permute-start | bytes 1105928 | tf_op jit(solution)/shard_map/ppermute | solution.py:215
  26.1 0.1 select_reduce_fusion.2.starts
  26.2 0.1 broadcast_in_dim.35.tall
  26.3 0.0 copy-start.2
  26.3 1.0 %copy-done.2 = bf16[45,32,128]{2,1,0:T(8,128)(2,1)S(1)} copy-done((bf16[45,32,128]{2,1,0:T(8,128)(2,1)S(1)}, bf16[45,32,128]{2,1,0:T(8,128)(2,1)}, u32[]{:S(2)}) %copy-start.2) | copy-done | bytes 368664
  27.3 1.3 %pack_near.1.packed.near_packed = bf16[3584,128]{1,0:T(8,128)(2,1)S(1)} custom-call(s32[13]{0:T(128)S(1)} %select_reduce_fusion.2.starts, bf16[128,128]{1,0:T(8,128)(2,1)S(1)} %and_convert_fusion.sort, s32[128,128]{1,0:T(8,128)S(1)} %broadcast_in_dim.35.tall, bf16[45,32,128]{2,1,0:T(8,128)(2,1)S(1)} %copy-done.2, ...), custom_call_target="tpu_custom_call" | custom-call | flops 1024 | bytes 1024 | tf_op jit(solution)/shard_map/pack_near/pallas_call | solution.py:248
  28.5 0.0 collective-permute-done.2.qb.q1b
  28.5 0.1 broadcast_in_dim.33.lens
  28.6 4.5 %early.1.old = f32[32,2048]{1,0:T(8,128)S(1)} custom-call(s32[13]{0:T(128)S(1)} %select_reduce_fusion.2.starts, s32[32,128]{1,0:T(8,128)S(1)} %broadcast_in_dim.33.lens, bf16[3584,128]{1,0:T(8,128)(2,1)S(1)} %pack_near.1.packed.near_packed, bf16[32,32,128]{2,1,0:T(8,128)(2,1)S(1)} %collective-permute-done.1.qa.q1a, ...), custom_call_target="tpu_custom_call" | custom-call | flops 1024 | bytes 1024 | tf_op jit(solution)/shard_map/early/pallas_call | solution.py:248
  33.1 0.0 collective-permute-done.4
  33.1 0.0 collective-permute-done.3
  33.1 0.1 add.68.qa.q2a
  33.2 0.1 collective-permute-start.6
  33.3 0.0 collective-permute-done.7.far
  33.3 2.3 %middle.1 = (bf16[2048,128]{1,0:T(8,128)(2,1)S(1)}, f32[32,2048]{1,0:T(8,128)S(1)}) custom-call(s32[13]{0:T(128)S(1)} %select_reduce_fusion.2.starts, s32[32,128]{1,0:T(8,128)S(1)} %broadcast_in_dim.33.lens, bf16[128,128]{1,0:T(8,128)(2,1)S(1)} %and_convert_fusion.sort, s32[128,128]{1,0:T(8,128)S(1)} %broadcast_in_dim.35.tall, ...), custom_call_target="tpu_custom_call" | custom-call | flops 1024 | bytes 1024 | tf_op jit(solution)/shard_map/middle/pallas_call | solution.py:248
  35.7 0.0 collective-permute-done.6.qb.q2b
  35.7 5.9 %second.1.old2 = f32[32,2048]{1,0:T(8,128)S(1)} custom-call(s32[13]{0:T(128)S(1)} %select_reduce_fusion.2.starts, s32[32,128]{1,0:T(8,128)S(1)} %broadcast_in_dim.33.lens, bf16[3584,128]{1,0:T(8,128)(2,1)S(1)} %pack_near.1.packed.near_packed, bf16[2048,128]{1,0:T(8,128)(2,1)S(1)} %get-tuple-element.24.far_packed, bf16[32,32,128]{2,1,0:T(8,128)(2,1)S(1)} %add.68.qa.q2a, ...), custom_call_target="tpu_custom_call" | custom-call | flops 1024 | bytes 1024 | tf_op jit(solution)/shard_map/second/pallas_call | solution.py:248
  41.6 0.0 collective-permute-done.far
  41.6 2.7 %late.1 = f32[32,128]{1,0:T(8,128)S(1)} custom-call(s32[13]{0:T(128)S(1)} %select_reduce_fusion.2.starts, s32[32]{0:T(128)S(1)} %get-tuple-element.25.order, s32[32,128]{1,0:T(8,128)S(1)} %broadcast_in_dim.33.lens, bf16[128,128]{1,0:T(8,128)(2,1)S(1)} %and_convert_fusion.sort, s32[128,128]{1,0:T(8,128)S(1)} %broadcast_in_dim.35.tall, ...), custom_call_target="tpu_custom_call" | custom-call | flops 1024 | bytes 1024 | tf_op jit(solution)/shard_map/late/pallas_call | solution.py:248
  44.3 0.1 collective-permute-start.8
  44.4 1.2 %collective-permute-done.8 = f32[32,128]{1,0:T(8,128)S(1)} collective-permute-done((f32[32,128]{1,0:T(8,128)S(1)}, f32[32,128]{1,0:T(8,128)S(1)}, u32[]{:S(2)}, u32[]{:S(2)}) %collective-permute-start.8) | collective-permute-done | bytes 16416 | tf_op jit(solution)/shard_map/ppermute | solution.py:215
  45.5 0.1 slice_select_fusion
  45.6 1.9 %collective-permute-start.9 = (f32[64,64]{1,0:T(8,128)S(1)}, f32[64,64]{1,0:T(8,128)S(1)}, u32[]{:S(2)}, u32[]{:S(2)}) collective-permute-start(f32[64,64]{1,0:T(8,128)S(1)} %slice_select_fusion), channel_id=1, source_target_pairs={{0,4},{1,9},{2,6},{3,11},{4,8},{5,13},{6,10},{7,15},{8,12},{9,17},... | collective-permute-start | bytes 49160 | tf_op jit(solution)/shard_map/ppermute | solution.py:225
  47.5 2.1 %collective-permute-start.10 = (f32[64,64]{1,0:T(8,128)S(1)}, f32[64,64]{1,0:T(8,128)S(1)}, u32[]{:S(2)}, u32[]{:S(2)}) collective-permute-start(f32[64,64]{1,0:T(8,128)S(1)} %slice_select_fusion), channel_id=1, source_target_pairs={{0,6},{1,11},{2,4},{3,9},{4,10},{5,15},{6,8},{7,13},{8,14},{9,19},... | collective-permute-start | bytes 49160 | tf_op jit(solution)/shard_map/ppermute | solution.py:225
  49.7 3.9 %collective-permute-done.9 = f32[64,64]{1,0:T(8,128)S(1)} collective-permute-done((f32[64,64]{1,0:T(8,128)S(1)}, f32[64,64]{1,0:T(8,128)S(1)}, u32[]{:S(2)}, u32[]{:S(2)}) %collective-permute-start.9) | collective-permute-done | bytes 16416 | tf_op jit(solution)/shard_map/ppermute | solution.py:225
  53.6 3.1 %collective-permute-done.10 = f32[64,64]{1,0:T(8,128)S(1)} collective-permute-done((f32[64,64]{1,0:T(8,128)S(1)}, f32[64,64]{1,0:T(8,128)S(1)}, u32[]{:S(2)}, u32[]{:S(2)}) %collective-permute-start.10) | collective-permute-done | bytes 16416 | tf_op jit(solution)/shard_map/ppermute | solution.py:225
  56.8 2.1 %collective-permute-start.11 = (f32[128,64]{1,0:T(8,128)S(1)}, f32[128,64]{1,0:T(8,128)S(1)}, u32[]{:S(2)}, u32[]{:S(2)}) collective-permute-start(f32[128,64]{1,0:T(8,128)S(1)} %maximum_select_fusion.2), channel_id=1, source_target_pairs={{0,1},{1,0},{2,3},{3,2},{4,5},{5,4},{6,7},{7,6},{8,9},{9,8},{10,11... | collective-permute-start | bytes 98312 | tf_op jit(solution)/shard_map/ppermute | solution.py:215
  58.9 0.9 %collective-permute-done.11 = f32[128,64]{1,0:T(8,128)S(1)} collective-permute-done((f32[128,64]{1,0:T(8,128)S(1)}, f32[128,64]{1,0:T(8,128)S(1)}, u32[]{:S(2)}, u32[]{:S(2)}) %collective-permute-start.11) | collective-permute-done | bytes 32800 | tf_op jit(solution)/shard_map/ppermute | solution.py:215
  59.8 0.7 %copy.6 = f32[64,2,128]{2,1,0:T(2,128)} copy(f32[64,2,128]{0,2,1:T(8,128)S(1)} %fusion) | data formatting | bytes 131072 | tf_op jit(solution)/shard_map/transpose | solution.py:337
  (11 shorter events, 0.1 us)
Async XLA Ops:
  0.0 1.0 %copy-start = (bf16[64,32,128]{2,1,0:T(8,128)(2,1)S(1)}, bf16[64,32,128]{2,1,0:T(8,128)(2,1)}, u32[]{:S(2)}) copy-start(bf16[64,32,128]{2,1,0:T(8,128)(2,1)} %param.4) | copy-start | bytes 1572868
  0.0 21.9 %copy-start.3 = (s32[4]{0:T(128)S(1)}, s32[4]{0:T(128)}, u32[]{:S(2)}) copy-start(s32[4]{0:T(128)} %constant.75.clone) | copy-start | bytes 52
  1.7 11.1 %copy-start.1 = (bf16[32,32,128]{2,1,0:T(8,128)(2,1)}, bf16[32,32,128]{2,1,0:T(8,128)(2,1)S(1)}, u32[]{:S(2)}) copy-start(bf16[32,32,128]{2,1,0:T(8,128)(2,1)S(1)} %prepare.1.after_ref) | copy-start | bytes 786436
  1.7 20.5 %collective-permute-start.1 = (bf16[32,32,128]{2,1,0:T(8,128)(2,1)S(1)}, bf16[32,32,128]{2,1,0:T(8,128)(2,1)S(1)}, u32[]{:S(2)}, u32[]{:S(2)}) collective-permute-start(bf16[32,32,128]{2,1,0:T(8,128)(2,1)S(1)} %prepare.1.after_ref), channel_id=1, source_target_pairs={{0,252},{1,255},{2,254},{3,253},{4,0},{5,1},{6,2},{7,3},{8,4},{9,5... | collective-permute-start | bytes 786440 | tf_op jit(solution)/shard_map/ppermute | solution.py:211
  15.3 8.7 %collective-permute-start.5 = (bf16[45,32,128]{2,1,0:T(8,128)(2,1)}, bf16[45,32,128]{2,1,0:T(8,128)(2,1)S(1)}, u32[]{:S(2)}, u32[]{:S(2)}) collective-permute-start(bf16[45,32,128]{2,1,0:T(8,128)(2,1)} %get-tuple-element.19), channel_id=1, source_target_pairs={{0,1},{1,0},{2,3},{3,2},{4,5},{5,4},{6,7},{7,6},{8,9},{9,8},{10,11... | collective-permute-start | bytes 1105928 | tf_op jit(solution)/shard_map/ppermute | solution.py:215
  15.4 17.7 %collective-permute-start.4 = (bf16[32,32,128]{2,1,0:T(8,128)(2,1)}, bf16[32,32,128]{2,1,0:T(8,128)(2,1)S(1)}, u32[]{:S(2)}, u32[]{:S(2)}) collective-permute-start(bf16[32,32,128]{2,1,0:T(8,128)(2,1)} %copy-done.1), channel_id=1, source_target_pairs={{0,248},{1,251},{2,250},{3,249},{4,252},{5,255},{6,254},{7,253},{3... | collective-permute-start | bytes 786440 | tf_op jit(solution)/shard_map/ppermute | solution.py:211
  19.5 13.8 %collective-permute-start.7 = (bf16[45,32,128]{2,1,0:T(8,128)(2,1)}, bf16[45,32,128]{2,1,0:T(8,128)(2,1)S(1)}, u32[]{:S(2)}, u32[]{:S(2)}) collective-permute-start(bf16[45,32,128]{2,1,0:T(8,128)(2,1)} %get-tuple-element.21), channel_id=1, source_target_pairs={{0,3},{1,2},{2,1},{3,0},{4,7},{5,6},{6,5},{7,4},{8,11},{9,10},{10,... | collective-permute-start | bytes 1105928 | tf_op jit(solution)/shard_map/ppermute | solution.py:215
  22.2 6.3 %collective-permute-start.2 = (bf16[32,32,128]{2,1,0:T(8,128)(2,1)S(1)}, bf16[32,32,128]{2,1,0:T(8,128)(2,1)S(1)}, u32[]{:S(2)}, u32[]{:S(2)}) collective-permute-start(bf16[32,32,128]{2,1,0:T(8,128)(2,1)S(1)} %collective-permute-done.1.qa.q1a), channel_id=1, source_target_pairs={{0,1},{1,0},{2,3},{3,2},{4,5},{5,4},{6,7},{7,6},{8,9},{9,8},{10,11... | collective-permute-start | bytes 786440 | tf_op jit(solution)/shard_map/ppermute | solution.py:215
  22.2 10.9 %collective-permute-start.3 = (bf16[32,32,128]{2,1,0:T(8,128)(2,1)S(1)}, bf16[32,32,128]{2,1,0:T(8,128)(2,1)S(1)}, u32[]{:S(2)}, u32[]{:S(2)}) collective-permute-start(bf16[32,32,128]{2,1,0:T(8,128)(2,1)S(1)} %collective-permute-done.1.qa.q1a), channel_id=1, source_target_pairs={{4,0},{5,1},{6,2},{7,3},{8,4},{9,5},{10,6},{11,7},{12,8},{13,9},{1... | collective-permute-start | bytes 786440 | tf_op jit(solution)/shard_map/ppermute | solution.py:211
  24.0 17.6 %collective-permute-start = (bf16[45,32,128]{2,1,0:T(8,128)(2,1)}, bf16[45,32,128]{2,1,0:T(8,128)(2,1)S(1)}, u32[]{:S(2)}, u32[]{:S(2)}) collective-permute-start(bf16[45,32,128]{2,1,0:T(8,128)(2,1)} %get-tuple-element.15), channel_id=1, source_target_pairs={{0,2},{1,3},{2,0},{3,1},{4,6},{5,7},{6,4},{7,5},{8,10},{9,11},{10,... | collective-permute-start | bytes 1105928 | tf_op jit(solution)/shard_map/ppermute | solution.py:215
  26.3 1.0 %copy-start.2 = (bf16[45,32,128]{2,1,0:T(8,128)(2,1)S(1)}, bf16[45,32,128]{2,1,0:T(8,128)(2,1)}, u32[]{:S(2)}) copy-start(bf16[45,32,128]{2,1,0:T(8,128)(2,1)} %get-tuple-element.18.own) | copy-start | bytes 1105924
  33.2 2.5 %collective-permute-start.6 = (bf16[32,32,128]{2,1,0:T(8,128)(2,1)S(1)}, bf16[32,32,128]{2,1,0:T(8,128)(2,1)S(1)}, u32[]{:S(2)}, u32[]{:S(2)}) collective-permute-start(bf16[32,32,128]{2,1,0:T(8,128)(2,1)S(1)} %add.68.qa.q2a), channel_id=1, source_target_pairs={{0,1},{1,0},{2,3},{3,2},{4,5},{5,4},{6,7},{7,6},{8,9},{9,8},{10,11... | collective-permute-start | bytes 786440 | tf_op jit(solution)/shard_map/ppermute | solution.py:215
  44.3 1.3 %collective-permute-start.8 = (f32[32,128]{1,0:T(8,128)S(1)}, f32[32,128]{1,0:T(8,128)S(1)}, u32[]{:S(2)}, u32[]{:S(2)}) collective-permute-start(f32[32,128]{1,0:T(8,128)S(1)} %late.1), channel_id=1, source_target_pairs={{0,1},{1,0},{2,3},{3,2},{4,5},{5,4},{6,7},{7,6},{8,9},{9,8},{10,11... | collective-permute-start | bytes 49160 | tf_op jit(solution)/shard_map/ppermute | solution.py:215
  45.6 8.0 %collective-permute-start.9 = (f32[64,64]{1,0:T(8,128)S(1)}, f32[64,64]{1,0:T(8,128)S(1)}, u32[]{:S(2)}, u32[]{:S(2)}) collective-permute-start(f32[64,64]{1,0:T(8,128)S(1)} %slice_select_fusion), channel_id=1, source_target_pairs={{0,4},{1,9},{2,6},{3,11},{4,8},{5,13},{6,10},{7,15},{8,12},{9,17},... | collective-permute-start | bytes 49160 | tf_op jit(solution)/shard_map/ppermute | solution.py:225
  47.5 9.2 %collective-permute-start.10 = (f32[64,64]{1,0:T(8,128)S(1)}, f32[64,64]{1,0:T(8,128)S(1)}, u32[]{:S(2)}, u32[]{:S(2)}) collective-permute-start(f32[64,64]{1,0:T(8,128)S(1)} %slice_select_fusion), channel_id=1, source_target_pairs={{0,6},{1,11},{2,4},{3,9},{4,10},{5,15},{6,8},{7,13},{8,14},{9,19},... | collective-permute-start | bytes 49160 | tf_op jit(solution)/shard_map/ppermute | solution.py:225
  56.8 3.0 %collective-permute-start.11 = (f32[128,64]{1,0:T(8,128)S(1)}, f32[128,64]{1,0:T(8,128)S(1)}, u32[]{:S(2)}, u32[]{:S(2)}) collective-permute-start(f32[128,64]{1,0:T(8,128)S(1)} %maximum_select_fusion.2), channel_id=1, source_target_pairs={{0,1},{1,0},{2,3},{3,2},{4,5},{5,4},{6,7},{7,6},{8,9},{9,8},{10,11... | collective-permute-start | bytes 98312 | tf_op jit(solution)/shard_map/ppermute | solution.py:215

commit v4 on v3

--- a/solution.py
+++ b/solution.py
@@ -197,10 +197,6 @@
     lax.fori_loop(0, docs, unsort, 0, unroll=8)
 
 
-def wraps(dp, shift):
-    return dp % RUN < shift
-
-
 def handed_back(block, shift, chosen=lambda dp: True):
     dp_size, tok_size = lax.axis_size("dp"), lax.axis_size("tok")
     route = []
@@ -272,7 +268,7 @@
         name="cut",
     )(jnp.transpose(documents, (1, 0, 2)), prepared)
     own, prepared = lax.optimization_barrier((slabs[0], prepared))
-    relayed = handed_back(arrived, 1, lambda i: not wraps(i + 1, 2)) + handed_back(prepared, 2, lambda i: wraps(i, 2))
+    relayed = handed_back(arrived, 1, lambda i: i % RUN != 0) + handed_back(prepared, 2, lambda i: i % RUN == 1)
     near, *fars = [swapped(slabs[n], SLABS[n]) for n in (1, 2, 3)]
 
     lens = lax.dynamic_slice_in_dim(lengths, dp * dcount + tok * mine, mine, 0)
@@ -309,12 +305,12 @@
         functools.partial(early_kernel, **shapes), "early", best_shape, [tops(2)], (starts,),
         wide_lens, near_packed, *pair,
     )
-    relayed, best = lax.optimization_barrier((relayed, best))
-    last_pair = (relayed, swapped(relayed, 1))
     far_packed, best = call(
         functools.partial(middle_kernel, **shapes), "middle", (packed_shape(1), best_shape), [tops(1)], (starts,),
         wide_lens, sort, tall, fars[0], *pair, best,
     )
+    relayed, best = lax.optimization_barrier((relayed, best))
+    last_pair = (relayed, swapped(relayed, 1))
     second = call(
         functools.partial(second_kernel, **shapes), "second", best_shape, [tops(2), tops(1)], (starts,),
         wide_lens, near_packed, far_packed, *last_pair,

time: 60.5 us -> 60.9 us (level)
  waiting for transfers between devices: 9.17 us -> 10.9 us
  Pallas kernels: 19.8 us -> 18.8 us
    ppermute x3, starting transfers between devices: 16.4 us -> 13.1 us  [handed_back(): return lax.ppermute(block, ('dp', 'tok'), route)]
    ppermute x2, starting transfers between devices: 4.03 us -> 7 us  [returned(): return lax.ppermute(block, ('dp', 'tok'), route)]
    pallas_call x6, Pallas kernels: 17.3 us -> 16.3 us  [call(): pl.pallas_call(kernel, out_shape=out_shape, in_specs=[SMEM] * len(scalars...]
    ppermute x2, waiting for transfers between devices: 7.1 us -> 7.98 us  [returned(): return lax.ppermute(block, ('dp', 'tok'), route)]
    ppermute x7, waiting for transfers between devices: 2.07 us -> 2.9 us  [swapped(): lax.ppermute(block, 'tok', [(i, i ^ mask) for i in range(lax.axis_size('t...]
  transfers between devices with their start and end apart: 12 -> 12, of which waited for: 4 -> 5; matrix products, arithmetic and copies ran while one was open for 3% -> 3% of each run, Pallas kernels for 27% -> 26%
where the time goes in v4:
time: 60.9 us; the launch traced here: 60.8 us
  starting transfers between devices  26.1 us (43%)
  Pallas kernels  18.8 us (31%)
  waiting for transfers between devices  10.9 us (18%)
  local copies, waits for them, and re-layouts  4.04 us (7%)
  other arithmetic  0.87 us (1%)
    pallas_call x6, Pallas kernels, call(): pl.pallas_call(kernel, out_shape=out_shape, in_specs=[SMEM] * len(scalars...  16.3 us
    ppermute x3, starting transfers between devices, handed_back(): return lax.ppermute(block, ('dp', 'tok'), route)  13.1 us
    ppermute x2, waiting for transfers between devices, returned(): return lax.ppermute(block, ('dp', 'tok'), route)  7.98 us
    ppermute x2, starting transfers between devices, returned(): return lax.ppermute(block, ('dp', 'tok'), route)  7 us
    ppermute x7, starting transfers between devices, swapped(): lax.ppermute(block, 'tok', [(i, i ^ mask) for i in range(lax.axis_size('t...  5.97 us
    ppermute x7, waiting for transfers between devices, swapped(): lax.ppermute(block, 'tok', [(i, i ^ mask) for i in range(lax.axis_size('t...  2.9 us
    pallas_call x1, Pallas kernels, per_device(): pl.pallas_call(cut_kernel, out_shape=(jax.ShapeDtypeStruct((slots, mine,...  2.5 us
    unnamed x8, local copies, waits for them, and re-layouts  2.04 us
  transfers between devices with their start and end apart: 12, of which 5 were waited for; matrix products, arithmetic and copies ran while one was open for 3% of the time, Pallas kernels for 26%

profile of v4, /device:TPU:1, one launch (start us, length us, event | category | flops | bytes accessed | tf_op | source)
XLA Modules:
  0.0 60.8 jit_solution(10897400909660694122)
XLA Ops:
  0.0 0.0 copy-start
  0.0 0.0 copy-start.3
  0.0 1.0 %copy-done = bf16[64,32,128]{2,1,0:T(8,128)(2,1)S(1)} copy-done((bf16[64,32,128]{2,1,0:T(8,128)(2,1)S(1)}, bf16[64,32,128]{2,1,0:T(8,128)(2,1)}, u32[]{:S(2)}) %copy-start) | copy-done | bytes 524312
  1.1 0.6 prepare.1.after_ref
  1.7 0.0 copy-start.1
  1.7 11.1 %collective-permute-start.1 = (bf16[32,32,128]{2,1,0:T(8,128)(2,1)S(1)}, bf16[32,32,128]{2,1,0:T(8,128)(2,1)S(1)}, u32[]{:S(2)}, u32[]{:S(2)}) collective-permute-start(bf16[32,32,128]{2,1,0:T(8,128)(2,1)S(1)} %prepare.1.after_ref), channel_id=1, source_target_pairs={{0,252},{1,255},{2,254},{3,253},{4,0},{5,1},{6,2},{7,3},{8,4},{9,5... | collective-permute-start | bytes 786440 | tf_op jit(solution)/shard_map/ppermute | solution.py:207
  12.8 0.0 copy-done.1
  12.8 2.5 %cut.1 = (bf16[45,32,128]{2,1,0:T(8,128)(2,1)}, bf16[45,32,128]{2,1,0:T(8,128)(2,1)}, bf16[45,32,128]{2,1,0:T(8,128)(2,1)}, bf16[45,32,128]{2,1,0:T(8,128)(2,1)}) custom-call(bf16[45,128,128]{2,1,0:T(8,128)(2,1)} %bitcast.7, bf16[32,32,128]{2,1,0:T(8,128)(2,1)} %copy-done.1), custom_call_target="tpu_custom_call" | custom-call | flops 1024 | bytes 1024 | tf_op jit(solution)/shard_map/cut/pallas_call | solution.py:260
  15.3 0.7 %collective-permute-start.4 = (bf16[32,32,128]{2,1,0:T(8,128)(2,1)}, bf16[32,32,128]{2,1,0:T(8,128)(2,1)S(1)}, u32[]{:S(2)}, u32[]{:S(2)}) collective-permute-start(bf16[32,32,128]{2,1,0:T(8,128)(2,1)} %copy-done.1), channel_id=1, source_target_pairs={{4,252},{5,255},{6,254},{7,253},{36,28},{37,29},{38,30},{39,31},{6... | collective-permute-start | bytes 786440 | tf_op jit(solution)/shard_map/ppermute | solution.py:207
  16.0 2.1 %collective-permute-start.5 = (bf16[45,32,128]{2,1,0:T(8,128)(2,1)}, bf16[45,32,128]{2,1,0:T(8,128)(2,1)S(1)}, u32[]{:S(2)}, u32[]{:S(2)}) collective-permute-start(bf16[45,32,128]{2,1,0:T(8,128)(2,1)} %get-tuple-element.18), channel_id=1, source_target_pairs={{0,3},{1,2},{2,1},{3,0},{4,7},{5,6},{6,5},{7,4},{8,11},{9,10},{10,... | collective-permute-start | bytes 1105928 | tf_op jit(solution)/shard_map/ppermute | solution.py:211
  18.1 0.0 collective-permute-start.6
  18.1 0.0 copy-done.3
  18.1 0.8 %dynamic_slice.6 = s32[32]{0:T(128)S(1)} dynamic-slice(s32[8192]{0:T(1024)} %param.6, s32[]{:T(128)S(6)} %select_n.101), dynamic_slice_sizes={32} | dynamic-slice | bytes 260 | tf_op jit(solution)/shard_map/dynamic_slice | solution.py:274
  18.9 0.2 convert_reduce_fusion
  19.1 0.1 eq.33
  19.2 0.1 and_convert_fusion.sort
  19.3 0.1 broadcast_add_fusion
  19.4 0.0 collective-permute-done.1.qa.q1a
  19.4 1.3 %collective-permute-start.3 = (bf16[32,32,128]{2,1,0:T(8,128)(2,1)S(1)}, bf16[32,32,128]{2,1,0:T(8,128)(2,1)S(1)}, u32[]{:S(2)}, u32[]{:S(2)}) collective-permute-start(bf16[32,32,128]{2,1,0:T(8,128)(2,1)S(1)} %collective-permute-done.1.qa.q1a), channel_id=1, source_target_pairs={{4,0},{5,1},{6,2},{7,3},{8,4},{9,5},{10,6},{11,7},{12,8},{13,9},{1... | collective-permute-start | bytes 786440 | tf_op jit(solution)/shard_map/ppermute | solution.py:207
  20.7 0.6 collective-permute-start.2
  21.3 0.1 select_reduce_fusion
  21.4 0.1 add.65
  21.4 0.1 slice.13
  21.5 0.1 broadcast_in_dim.34
  21.6 0.1 convert_reduce_fusion.1
  21.7 0.0 collective-permute-done.6.near
  21.7 0.9 %collective-permute-start = (bf16[45,32,128]{2,1,0:T(8,128)(2,1)}, bf16[45,32,128]{2,1,0:T(8,128)(2,1)S(1)}, u32[]{:S(2)}, u32[]{:S(2)}) collective-permute-start(bf16[45,32,128]{2,1,0:T(8,128)(2,1)} %get-tuple-element.15), channel_id=1, source_target_pairs={{0,2},{1,3},{2,0},{3,1},{4,6},{5,7},{6,4},{7,5},{8,10},{9,11},{10,... | collective-permute-start | bytes 1105928 | tf_op jit(solution)/shard_map/ppermute | solution.py:211
  22.7 0.1 select_reduce_fusion.2.starts
  22.8 0.1 broadcast_in_dim.35.tall
  22.9 0.0 copy-start.2
  22.9 1.0 %copy-done.2 = bf16[45,32,128]{2,1,0:T(8,128)(2,1)S(1)} copy-done((bf16[45,32,128]{2,1,0:T(8,128)(2,1)S(1)}, bf16[45,32,128]{2,1,0:T(8,128)(2,1)}, u32[]{:S(2)}) %copy-start.2) | copy-done | bytes 368664
  23.9 1.3 %pack_near.1.packed.near_packed = bf16[3584,128]{1,0:T(8,128)(2,1)S(1)} custom-call(s32[13]{0:T(128)S(1)} %select_reduce_fusion.2.starts, bf16[128,128]{1,0:T(8,128)(2,1)S(1)} %and_convert_fusion.sort, s32[128,128]{1,0:T(8,128)S(1)} %broadcast_in_dim.35.tall, bf16[45,32,128]{2,1,0:T(8,128)(2,1)S(1)} %copy-done.2, ...), custom_call_target="tpu_custom_call" | custom-call | flops 1024 | bytes 1024 | tf_op jit(solution)/shard_map/pack_near/pallas_call | solution.py:244
  25.1 0.0 collective-permute-done.2.qb.q1b
  25.1 0.1 broadcast_in_dim.33.lens
  25.2 4.0 %early.1.old = f32[32,2048]{1,0:T(8,128)S(1)} custom-call(s32[13]{0:T(128)S(1)} %select_reduce_fusion.2.starts, s32[32,128]{1,0:T(8,128)S(1)} %broadcast_in_dim.33.lens, bf16[3584,128]{1,0:T(8,128)(2,1)S(1)} %pack_near.1.packed.near_packed, bf16[32,32,128]{2,1,0:T(8,128)(2,1)S(1)} %collective-permute-done.1.qa.q1a, ...), custom_call_target="tpu_custom_call" | custom-call | flops 1024 | bytes 1024 | tf_op jit(solution)/shard_map/early/pallas_call | solution.py:244
  29.3 0.0 collective-permute-done.5.far
  29.3 2.3 %middle.1 = (bf16[2048,128]{1,0:T(8,128)(2,1)S(1)}, f32[32,2048]{1,0:T(8,128)S(1)}) custom-call(s32[13]{0:T(128)S(1)} %select_reduce_fusion.2.starts, s32[32,128]{1,0:T(8,128)S(1)} %broadcast_in_dim.33.lens, bf16[128,128]{1,0:T(8,128)(2,1)S(1)} %and_convert_fusion.sort, s32[128,128]{1,0:T(8,128)S(1)} %broadcast_in_dim.35.tall, ...), custom_call_target="tpu_custom_call" | custom-call | flops 1024 | bytes 1024 | tf_op jit(solution)/shard_map/middle/pallas_call | solution.py:244
  31.6 0.0 collective-permute-done.4
  31.6 0.0 collective-permute-done.3
  31.6 0.1 add.68.qa.q2a
  31.7 0.6 %collective-permute-start.7 = (bf16[32,32,128]{2,1,0:T(8,128)(2,1)S(1)}, bf16[32,32,128]{2,1,0:T(8,128)(2,1)S(1)}, u32[]{:S(2)}, u32[]{:S(2)}) collective-permute-start(bf16[32,32,128]{2,1,0:T(8,128)(2,1)S(1)} %add.68.qa.q2a), channel_id=1, source_target_pairs={{0,1},{1,0},{2,3},{3,2},{4,5},{5,4},{6,7},{7,6},{8,9},{9,8},{10,11... | collective-permute-start | bytes 786440 | tf_op jit(solution)/shard_map/ppermute | solution.py:211
  32.4 1.2 %collective-permute-done.7.qb.q2b = bf16[32,32,128]{2,1,0:T(8,128)(2,1)S(1)} collective-permute-done((bf16[32,32,128]{2,1,0:T(8,128)(2,1)S(1)}, bf16[32,32,128]{2,1,0:T(8,128)(2,1)S(1)}, u32[]{:S(2)}, u32[]{:S(2)}) %collective-permute-start.7) | collective-permute-done | bytes 262176 | tf_op jit(solution)/shard_map/ppermute | solution.py:211
  33.5 5.5 %second.1.old2 = f32[32,2048]{1,0:T(8,128)S(1)} custom-call(s32[13]{0:T(128)S(1)} %select_reduce_fusion.2.starts, s32[32,128]{1,0:T(8,128)S(1)} %broadcast_in_dim.33.lens, bf16[3584,128]{1,0:T(8,128)(2,1)S(1)} %pack_near.1.packed.near_packed, bf16[2048,128]{1,0:T(8,128)(2,1)S(1)} %get-tuple-element.24.far_packed, bf16[32,32,128]{2,1,0:T(8,128)(2,1)S(1)} %add.68.qa.q2a, ...), custom_call_target="tpu_custom_call" | custom-call | flops 1024 | bytes 1024 | tf_op jit(solution)/shard_map/second/pallas_call | solution.py:244
  39.0 0.0 collective-permute-done.far
  39.0 2.6 %late.1 = f32[32,128]{1,0:T(8,128)S(1)} custom-call(s32[13]{0:T(128)S(1)} %select_reduce_fusion.2.starts, s32[32]{0:T(128)S(1)} %get-tuple-element.25.order, s32[32,128]{1,0:T(8,128)S(1)} %broadcast_in_dim.33.lens, bf16[128,128]{1,0:T(8,128)(2,1)S(1)} %and_convert_fusion.sort, s32[128,128]{1,0:T(8,128)S(1)} %broadcast_in_dim.35.tall, ...), custom_call_target="tpu_custom_call" | custom-call | flops 1024 | bytes 1024 | tf_op jit(solution)/shard_map/late/pallas_call | solution.py:244
  41.6 0.9 %collective-permute-start.8 = (f32[32,128]{1,0:T(8,128)S(1)}, f32[32,128]{1,0:T(8,128)S(1)}, u32[]{:S(2)}, u32[]{:S(2)}) collective-permute-start(f32[32,128]{1,0:T(8,128)S(1)} %late.1), channel_id=1, source_target_pairs={{0,1},{1,0},{2,3},{3,2},{4,5},{5,4},{6,7},{7,6},{8,9},{9,8},{10,11... | collective-permute-start | bytes 49160 | tf_op jit(solution)/shard_map/ppermute | solution.py:211
  42.4 0.8 %collective-permute-done.8 = f32[32,128]{1,0:T(8,128)S(1)} collective-permute-done((f32[32,128]{1,0:T(8,128)S(1)}, f32[32,128]{1,0:T(8,128)S(1)}, u32[]{:S(2)}, u32[]{:S(2)}) %collective-permute-start.8) | collective-permute-done | bytes 16416 | tf_op jit(solution)/shard_map/ppermute | solution.py:211
  43.3 0.1 slice_select_fusion
  43.4 7.0 %collective-permute-start.10 = (f32[64,64]{1,0:T(8,128)S(1)}, f32[64,64]{1,0:T(8,128)S(1)}, u32[]{:S(2)}, u32[]{:S(2)}) collective-permute-start(f32[64,64]{1,0:T(8,128)S(1)} %slice_select_fusion), channel_id=1, source_target_pairs={{0,6},{1,11},{2,4},{3,9},{4,10},{5,15},{6,8},{7,13},{8,14},{9,19},... | collective-permute-start | bytes 49160 | tf_op jit(solution)/shard_map/ppermute | solution.py:221
  50.4 0.0 collective-permute-start.9
  50.4 2.1 %collective-permute-done.10 = f32[64,64]{1,0:T(8,128)S(1)} collective-permute-done((f32[64,64]{1,0:T(8,128)S(1)}, f32[64,64]{1,0:T(8,128)S(1)}, u32[]{:S(2)}, u32[]{:S(2)}) %collective-permute-start.10) | collective-permute-done | bytes 16416 | tf_op jit(solution)/shard_map/ppermute | solution.py:221
  52.5 5.9 %collective-permute-done.9 = f32[64,64]{1,0:T(8,128)S(1)} collective-permute-done((f32[64,64]{1,0:T(8,128)S(1)}, f32[64,64]{1,0:T(8,128)S(1)}, u32[]{:S(2)}, u32[]{:S(2)}) %collective-permute-start.9) | collective-permute-done | bytes 16416 | tf_op jit(solution)/shard_map/ppermute | solution.py:221
  58.4 0.8 %collective-permute-start.11 = (f32[128,64]{1,0:T(8,128)S(1)}, f32[128,64]{1,0:T(8,128)S(1)}, u32[]{:S(2)}, u32[]{:S(2)}) collective-permute-start(f32[128,64]{1,0:T(8,128)S(1)} %maximum_select_fusion.2), channel_id=1, source_target_pairs={{0,1},{1,0},{2,3},{3,2},{4,5},{5,4},{6,7},{7,6},{8,9},{9,8},{10,11... | collective-permute-start | bytes 98312 | tf_op jit(solution)/shard_map/ppermute | solution.py:211
  59.2 0.9 %collective-permute-done.11 = f32[128,64]{1,0:T(8,128)S(1)} collective-permute-done((f32[128,64]{1,0:T(8,128)S(1)}, f32[128,64]{1,0:T(8,128)S(1)}, u32[]{:S(2)}, u32[]{:S(2)}) %collective-permute-start.11) | collective-permute-done | bytes 32800 | tf_op jit(solution)/shard_map/ppermute | solution.py:211
  60.1 0.7 %copy.6 = f32[64,2,128]{2,1,0:T(2,128)} copy(f32[64,2,128]{0,2,1:T(8,128)S(1)} %fusion) | data formatting | bytes 131072 | tf_op jit(solution)/shard_map/transpose | solution.py:333
  (11 shorter events, 0.1 us)
Async XLA Ops:
  0.0 1.0 %copy-start = (bf16[64,32,128]{2,1,0:T(8,128)(2,1)S(1)}, bf16[64,32,128]{2,1,0:T(8,128)(2,1)}, u32[]{:S(2)}) copy-start(bf16[64,32,128]{2,1,0:T(8,128)(2,1)} %param.4) | copy-start | bytes 1572868
  0.0 18.1 %copy-start.3 = (s32[4]{0:T(128)S(1)}, s32[4]{0:T(128)}, u32[]{:S(2)}) copy-start(s32[4]{0:T(128)} %constant.75.clone) | copy-start | bytes 52
  1.7 11.1 %copy-start.1 = (bf16[32,32,128]{2,1,0:T(8,128)(2,1)}, bf16[32,32,128]{2,1,0:T(8,128)(2,1)S(1)}, u32[]{:S(2)}) copy-start(bf16[32,32,128]{2,1,0:T(8,128)(2,1)S(1)} %prepare.1.after_ref) | copy-start | bytes 786436
  1.7 17.7 %collective-permute-start.1 = (bf16[32,32,128]{2,1,0:T(8,128)(2,1)S(1)}, bf16[32,32,128]{2,1,0:T(8,128)(2,1)S(1)}, u32[]{:S(2)}, u32[]{:S(2)}) collective-permute-start(bf16[32,32,128]{2,1,0:T(8,128)(2,1)S(1)} %prepare.1.after_ref), channel_id=1, source_target_pairs={{0,252},{1,255},{2,254},{3,253},{4,0},{5,1},{6,2},{7,3},{8,4},{9,5... | collective-permute-start | bytes 786440 | tf_op jit(solution)/shard_map/ppermute | solution.py:207
  15.3 16.3 %collective-permute-start.4 = (bf16[32,32,128]{2,1,0:T(8,128)(2,1)}, bf16[32,32,128]{2,1,0:T(8,128)(2,1)S(1)}, u32[]{:S(2)}, u32[]{:S(2)}) collective-permute-start(bf16[32,32,128]{2,1,0:T(8,128)(2,1)} %copy-done.1), channel_id=1, source_target_pairs={{4,252},{5,255},{6,254},{7,253},{36,28},{37,29},{38,30},{39,31},{6... | collective-permute-start | bytes 786440 | tf_op jit(solution)/shard_map/ppermute | solution.py:207
  16.0 13.3 %collective-permute-start.5 = (bf16[45,32,128]{2,1,0:T(8,128)(2,1)}, bf16[45,32,128]{2,1,0:T(8,128)(2,1)S(1)}, u32[]{:S(2)}, u32[]{:S(2)}) collective-permute-start(bf16[45,32,128]{2,1,0:T(8,128)(2,1)} %get-tuple-element.18), channel_id=1, source_target_pairs={{0,3},{1,2},{2,1},{3,0},{4,7},{5,6},{6,5},{7,4},{8,11},{9,10},{10,... | collective-permute-start | bytes 1105928 | tf_op jit(solution)/shard_map/ppermute | solution.py:211
  18.1 3.6 %collective-permute-start.6 = (bf16[45,32,128]{2,1,0:T(8,128)(2,1)}, bf16[45,32,128]{2,1,0:T(8,128)(2,1)S(1)}, u32[]{:S(2)}, u32[]{:S(2)}) collective-permute-start(bf16[45,32,128]{2,1,0:T(8,128)(2,1)} %get-tuple-element.20), channel_id=1, source_target_pairs={{0,1},{1,0},{2,3},{3,2},{4,5},{5,4},{6,7},{7,6},{8,9},{9,8},{10,11... | collective-permute-start | bytes 1105928 | tf_op jit(solution)/shard_map/ppermute | solution.py:211
  19.4 12.2 %collective-permute-start.3 = (bf16[32,32,128]{2,1,0:T(8,128)(2,1)S(1)}, bf16[32,32,128]{2,1,0:T(8,128)(2,1)S(1)}, u32[]{:S(2)}, u32[]{:S(2)}) collective-permute-start(bf16[32,32,128]{2,1,0:T(8,128)(2,1)S(1)} %collective-permute-done.1.qa.q1a), channel_id=1, source_target_pairs={{4,0},{5,1},{6,2},{7,3},{8,4},{9,5},{10,6},{11,7},{12,8},{13,9},{1... | collective-permute-start | bytes 786440 | tf_op jit(solution)/shard_map/ppermute | solution.py:207
  20.7 4.5 %collective-permute-start.2 = (bf16[32,32,128]{2,1,0:T(8,128)(2,1)S(1)}, bf16[32,32,128]{2,1,0:T(8,128)(2,1)S(1)}, u32[]{:S(2)}, u32[]{:S(2)}) collective-permute-start(bf16[32,32,128]{2,1,0:T(8,128)(2,1)S(1)} %collective-permute-done.1.qa.q1a), channel_id=1, source_target_pairs={{0,1},{1,0},{2,3},{3,2},{4,5},{5,4},{6,7},{7,6},{8,9},{9,8},{10,11... | collective-permute-start | bytes 786440 | tf_op jit(solution)/shard_map/ppermute | solution.py:211
  21.7 17.3 %collective-permute-start = (bf16[45,32,128]{2,1,0:T(8,128)(2,1)}, bf16[45,32,128]{2,1,0:T(8,128)(2,1)S(1)}, u32[]{:S(2)}, u32[]{:S(2)}) collective-permute-start(bf16[45,32,128]{2,1,0:T(8,128)(2,1)} %get-tuple-element.15), channel_id=1, source_target_pairs={{0,2},{1,3},{2,0},{3,1},{4,6},{5,7},{6,4},{7,5},{8,10},{9,11},{10,... | collective-permute-start | bytes 1105928 | tf_op jit(solution)/shard_map/ppermute | solution.py:211
  22.9 1.0 %copy-start.2 = (bf16[45,32,128]{2,1,0:T(8,128)(2,1)S(1)}, bf16[45,32,128]{2,1,0:T(8,128)(2,1)}, u32[]{:S(2)}) copy-start(bf16[45,32,128]{2,1,0:T(8,128)(2,1)} %get-tuple-element.19.own) | copy-start | bytes 1105924
  31.7 1.8 %collective-permute-start.7 = (bf16[32,32,128]{2,1,0:T(8,128)(2,1)S(1)}, bf16[32,32,128]{2,1,0:T(8,128)(2,1)S(1)}, u32[]{:S(2)}, u32[]{:S(2)}) collective-permute-start(bf16[32,32,128]{2,1,0:T(8,128)(2,1)S(1)} %add.68.qa.q2a), channel_id=1, source_target_pairs={{0,1},{1,0},{2,3},{3,2},{4,5},{5,4},{6,7},{7,6},{8,9},{9,8},{10,11... | collective-permute-start | bytes 786440 | tf_op jit(solution)/shard_map/ppermute | solution.py:211
  41.6 1.7 %collective-permute-start.8 = (f32[32,128]{1,0:T(8,128)S(1)}, f32[32,128]{1,0:T(8,128)S(1)}, u32[]{:S(2)}, u32[]{:S(2)}) collective-permute-start(f32[32,128]{1,0:T(8,128)S(1)} %late.1), channel_id=1, source_target_pairs={{0,1},{1,0},{2,3},{3,2},{4,5},{5,4},{6,7},{7,6},{8,9},{9,8},{10,11... | collective-permute-start | bytes 49160 | tf_op jit(solution)/shard_map/ppermute | solution.py:211
  43.4 9.1 %collective-permute-start.10 = (f32[64,64]{1,0:T(8,128)S(1)}, f32[64,64]{1,0:T(8,128)S(1)}, u32[]{:S(2)}, u32[]{:S(2)}) collective-permute-start(f32[64,64]{1,0:T(8,128)S(1)} %slice_select_fusion), channel_id=1, source_target_pairs={{0,6},{1,11},{2,4},{3,9},{4,10},{5,15},{6,8},{7,13},{8,14},{9,19},... | collective-permute-start | bytes 49160 | tf_op jit(solution)/shard_map/ppermute | solution.py:221
  50.4 8.0 %collective-permute-start.9 = (f32[64,64]{1,0:T(8,128)S(1)}, f32[64,64]{1,0:T(8,128)S(1)}, u32[]{:S(2)}, u32[]{:S(2)}) collective-permute-start(f32[64,64]{1,0:T(8,128)S(1)} %slice_select_fusion), channel_id=1, source_target_pairs={{0,4},{1,9},{2,6},{3,11},{4,8},{5,13},{6,10},{7,15},{8,12},{9,17},... | collective-permute-start | bytes 49160 | tf_op jit(solution)/shard_map/ppermute | solution.py:221
  58.4 1.7 %collective-permute-start.11 = (f32[128,64]{1,0:T(8,128)S(1)}, f32[128,64]{1,0:T(8,128)S(1)}, u32[]{:S(2)}, u32[]{:S(2)}) collective-permute-start(f32[128,64]{1,0:T(8,128)S(1)} %maximum_select_fusion.2), channel_id=1, source_target_pairs={{0,1},{1,0},{2,3},{3,2},{4,5},{5,4},{6,7},{7,6},{8,9},{9,8},{10,11... | collective-permute-start | bytes 98312 | tf_op jit(solution)/shard_map/ppermute | solution.py:211

commit v5 on v3

--- a/solution.py
+++ b/solution.py
@@ -52,9 +52,9 @@
     *slab_refs, sems = refs
     mine = slab_refs[0].shape[1]
     cuts = []
-    for n in (2, 3, 1, 0):
+    for n in (2, 3, 1):
         first = pl.multiple_of((lax.axis_index("tok") ^ SLABS[n]) * mine, mine)
-        cuts.append(pltpu.make_async_copy(docs_ref.at[:, pl.ds(first, mine), :], slab_refs[n], sems.at[n]))
+        cuts.append(pltpu.make_async_copy(docs_ref.at[:, pl.ds(first, mine), :], slab_refs[n - 1], sems.at[n]))
         cuts[-1].start()
     for cut in cuts:
         cut.wait()
@@ -261,21 +261,26 @@
         [pltpu.VMEM((half * tokens, width), f32)], (), lax.dynamic_slice_in_dim(queries, core * half, half, 0),
     )
     arrived = handed_back(prepared, 1)
-    slabs = pl.pallas_call(
+    by_slot = jnp.transpose(documents, (1, 0, 2))
+    cut = pl.pallas_call(
         cut_kernel,
-        out_shape=(jax.ShapeDtypeStruct((slots, mine, width), bf16),) * tok_size,
+        out_shape=(jax.ShapeDtypeStruct((slots, mine, width), bf16),) * (tok_size - 1),
         in_specs=[HBM, HBM],
-        out_specs=(VMEM,) * tok_size,
+        out_specs=(VMEM,) * (tok_size - 1),
         scratch_shapes=[pltpu.SemaphoreType.DMA((tok_size,))],
         compiler_params=pltpu.CompilerParams(vmem_limit_bytes=CUT_VMEM_LIMIT),
         cost_estimate=cost,
         name="cut",
-    )(jnp.transpose(documents, (1, 0, 2)), prepared)
-    own, prepared = lax.optimization_barrier((slabs[0], prepared))
+    )(by_slot, prepared)
+    slabs = [None, *cut]
+    sent_slab, prepared = lax.optimization_barrier((cut[0], prepared))
+    slabs[1] = sent_slab
+    own = lax.dynamic_slice_in_dim(by_slot, tok * mine, mine, 1)
     relayed = handed_back(arrived, 1, lambda i: not wraps(i + 1, 2)) + handed_back(prepared, 2, lambda i: wraps(i, 2))
     near, *fars = [swapped(slabs[n], SLABS[n]) for n in (1, 2, 3)]
 
     lens = lax.dynamic_slice_in_dim(lengths, dp * dcount + tok * mine, mine, 0)
+    lens, own = lax.optimization_barrier((lens, own))
     index = jnp.arange(mine, dtype=jnp.int32)
     ahead = (lens[None, :] > lens[:, None]) | ((lens[None, :] == lens[:, None]) & (index[None, :] < index[:, None]))
     rank = jnp.sum(ahead.astype(jnp.int32), axis=1)

time: 60.5 us -> 60.7 us (level)
  Pallas kernels: 19.8 us -> 16.9 us
  waiting for transfers between devices: 9.17 us -> 10.9 us
  starting transfers between devices: 26.4 us -> 27.5 us
    pallas_call x6, Pallas kernels: 17.3 us -> 14.6 us  [call(): pl.pallas_call(kernel, out_shape=out_shape, in_specs=[SMEM] * len(scalars...]
    ppermute x2, waiting for transfers between devices: 7.1 us -> 8.88 us  [returned(): return lax.ppermute(block, ('dp', 'tok'), route)]
    ppermute x7, starting transfers between devices: 5.97 us -> 7.7 us  [swapped(): lax.ppermute(block, 'tok', [(i, i ^ mask) for i in range(lax.axis_size('t...]
    dynamic_slice x0 -> x1, local copies, waits for them, and re-layouts: none -> 1.02 us  [per_device(): own = lax.dynamic_slice_in_dim(by_slot, tok * mine, mine, 1)]
    unnamed x8 -> x6, local copies, waits for them, and re-layouts: 2.04 us -> 1.05 us
    ppermute x2, starting transfers between devices: 4.03 us -> 3.4 us  [returned(): return lax.ppermute(block, ('dp', 'tok'), route)]
  transfers between devices with their start and end apart: 12 -> 12, of which waited for: 4 -> 5; matrix products, arithmetic and copies ran while one was open for 3% -> 5% of each run, Pallas kernels for 27% -> 23%
where the time goes in v5:
time: 60.7 us; the launch traced here: 60.5 us
  starting transfers between devices  27.5 us (45%)
  Pallas kernels  16.9 us (28%)
  waiting for transfers between devices  10.9 us (18%)
  local copies, waits for them, and re-layouts  4.06 us (7%)
  other arithmetic  0.87 us (1%)
    ppermute x3, starting transfers between devices, handed_back(): return lax.ppermute(block, ('dp', 'tok'), route)  16.4 us
    pallas_call x6, Pallas kernels, call(): pl.pallas_call(kernel, out_shape=out_shape, in_specs=[SMEM] * len(scalars...  14.6 us
    ppermute x2, waiting for transfers between devices, returned(): return lax.ppermute(block, ('dp', 'tok'), route)  8.88 us
    ppermute x7, starting transfers between devices, swapped(): lax.ppermute(block, 'tok', [(i, i ^ mask) for i in range(lax.axis_size('t...  7.7 us
    ppermute x2, starting transfers between devices, returned(): return lax.ppermute(block, ('dp', 'tok'), route)  3.4 us
    pallas_call x1, Pallas kernels, per_device(): pl.pallas_call(cut_kernel, out_shape=(jax.ShapeDtypeStruct((slots, mine,...  2.28 us
    ppermute x7, waiting for transfers between devices, swapped(): lax.ppermute(block, 'tok', [(i, i ^ mask) for i in range(lax.axis_size('t...  1.74 us
  transfers between devices with their start and end apart: 12, of which 5 were waited for; matrix products, arithmetic and copies ran while one was open for 5% of the time, Pallas kernels for 23%

profile of v5, /device:TPU:1, one launch (start us, length us, event | category | flops | bytes accessed | tf_op | source)
XLA Modules:
  0.0 60.5 jit_solution(10109001475904068771)
XLA Ops:
  0.0 0.0 copy-start
  0.0 1.0 %copy-done = bf16[64,32,128]{2,1,0:T(8,128)(2,1)S(1)} copy-done((bf16[64,32,128]{2,1,0:T(8,128)(2,1)S(1)}, bf16[64,32,128]{2,1,0:T(8,128)(2,1)}, u32[]{:S(2)}) %copy-start) | copy-done | bytes 524312
  1.1 0.0 copy-start.2
  1.1 0.6 prepare.1.after_ref
  1.7 0.0 copy-start.1
  1.7 11.1 %collective-permute-start.1 = (bf16[32,32,128]{2,1,0:T(8,128)(2,1)S(1)}, bf16[32,32,128]{2,1,0:T(8,128)(2,1)S(1)}, u32[]{:S(2)}, u32[]{:S(2)}) collective-permute-start(bf16[32,32,128]{2,1,0:T(8,128)(2,1)S(1)} %prepare.1.after_ref), channel_id=1, source_target_pairs={{0,252},{1,255},{2,254},{3,253},{4,0},{5,1},{6,2},{7,3},{8,4},{9,5... | collective-permute-start | bytes 786440 | tf_op jit(solution)/shard_map/ppermute | solution.py:211
  12.8 0.0 copy-done.1
  12.8 2.3 %cut.1 = (bf16[45,32,128]{2,1,0:T(8,128)(2,1)}, bf16[45,32,128]{2,1,0:T(8,128)(2,1)}, bf16[45,32,128]{2,1,0:T(8,128)(2,1)}) custom-call(bf16[45,128,128]{2,1,0:T(8,128)(2,1)} %bitcast.9, bf16[32,32,128]{2,1,0:T(8,128)(2,1)} %copy-done.1), custom_call_target="tpu_custom_call" | custom-call | flops 1024 | bytes 1024 | tf_op jit(solution)/shard_map/cut/pallas_call | solution.py:265
  15.1 0.1 collective-permute-start.5
  15.2 4.0 %collective-permute-start.4 = (bf16[32,32,128]{2,1,0:T(8,128)(2,1)}, bf16[32,32,128]{2,1,0:T(8,128)(2,1)S(1)}, u32[]{:S(2)}, u32[]{:S(2)}) collective-permute-start(bf16[32,32,128]{2,1,0:T(8,128)(2,1)} %copy-done.1), channel_id=1, source_target_pairs={{0,248},{1,251},{2,250},{3,249},{4,252},{5,255},{6,254},{7,253},{3... | collective-permute-start | bytes 786440 | tf_op jit(solution)/shard_map/ppermute | solution.py:211
  19.2 1.5 %collective-permute-start.7 = (bf16[45,32,128]{2,1,0:T(8,128)(2,1)}, bf16[45,32,128]{2,1,0:T(8,128)(2,1)S(1)}, u32[]{:S(2)}, u32[]{:S(2)}) collective-permute-start(bf16[45,32,128]{2,1,0:T(8,128)(2,1)} %get-tuple-element.23), channel_id=1, source_target_pairs={{0,3},{1,2},{2,1},{3,0},{4,7},{5,6},{6,5},{7,4},{8,11},{9,10},{10,... | collective-permute-start | bytes 1105928 | tf_op jit(solution)/shard_map/ppermute | solution.py:215
  20.7 1.0 %dynamic-slice_bitcast_fusion.own = bf16[45,32,128]{2,1,0:T(8,128)(2,1)S(1)} fusion(bf16[128,45,128]{2,0,1:T(8,128)(2,1)} %param.5, s32[]{:T(128)S(6)} %select_n.105), kind=kLoop, calls=%fused_computation | loop fusion | bytes 737284 | tf_op jit(solution)/shard_map/dynamic_slice | solution.py:278
  21.7 0.8 %dynamic_slice.9 = s32[32]{0:T(128)S(1)} dynamic-slice(s32[8192]{0:T(1024)} %param.6, s32[]{:T(128)S(6)} %select_n.104), dynamic_slice_sizes={32} | dynamic-slice | bytes 260 | tf_op jit(solution)/shard_map/dynamic_slice | solution.py:282
  22.5 0.2 convert_reduce_fusion
  22.7 0.0 copy-done.2
  22.7 0.1 eq.33
  22.8 0.1 and_convert_fusion.sort
  22.9 0.1 broadcast_add_fusion
  23.0 0.0 collective-permute-done.1.qa.q1a
  23.0 0.0 collective-permute-start.2
  23.0 1.3 %collective-permute-start.3 = (bf16[32,32,128]{2,1,0:T(8,128)(2,1)S(1)}, bf16[32,32,128]{2,1,0:T(8,128)(2,1)S(1)}, u32[]{:S(2)}, u32[]{:S(2)}) collective-permute-start(bf16[32,32,128]{2,1,0:T(8,128)(2,1)S(1)} %collective-permute-done.1.qa.q1a), channel_id=1, source_target_pairs={{4,0},{5,1},{6,2},{7,3},{8,4},{9,5},{10,6},{11,7},{12,8},{13,9},{1... | collective-permute-start | bytes 786440 | tf_op jit(solution)/shard_map/ppermute | solution.py:211
  24.3 0.1 select_reduce_fusion
  24.4 0.1 slice.13
  24.5 0.1 add.69
  24.6 0.1 broadcast_in_dim.34
  24.7 0.1 convert_reduce_fusion.1
  24.8 0.0 collective-permute-done.5.near
  24.8 2.1 %collective-permute-start = (bf16[45,32,128]{2,1,0:T(8,128)(2,1)}, bf16[45,32,128]{2,1,0:T(8,128)(2,1)S(1)}, u32[]{:S(2)}, u32[]{:S(2)}) collective-permute-start(bf16[45,32,128]{2,1,0:T(8,128)(2,1)} %get-tuple-element.17), channel_id=1, source_target_pairs={{0,2},{1,3},{2,0},{3,1},{4,6},{5,7},{6,4},{7,5},{8,10},{9,11},{10,... | collective-permute-start | bytes 1105928 | tf_op jit(solution)/shard_map/ppermute | solution.py:215
  26.9 0.1 select_reduce_fusion.2.starts
  27.0 0.1 broadcast_in_dim.35.tall
  27.1 1.3 %pack_near.1.packed.near_packed = bf16[3584,128]{1,0:T(8,128)(2,1)S(1)} custom-call(s32[13]{0:T(128)S(1)} %select_reduce_fusion.2.starts, bf16[128,128]{1,0:T(8,128)(2,1)S(1)} %and_convert_fusion.sort, s32[128,128]{1,0:T(8,128)S(1)} %broadcast_in_dim.35.tall, bf16[45,32,128]{2,1,0:T(8,128)(2,1)S(1)} %dynamic-slice_bitcast_fusion.own, ...), custom_call_target="tpu_custom_call" | custom-call | flops 1024 | bytes 1024 | tf_op jit(solution)/shard_map/pack_near/pallas_call | solution.py:248
  28.3 0.0 collective-permute-done.2.qb.q1b
  28.4 0.1 broadcast_in_dim.33.lens
  28.4 3.6 %early.1.old = f32[32,2048]{1,0:T(8,128)S(1)} custom-call(s32[13]{0:T(128)S(1)} %select_reduce_fusion.2.starts, s32[32,128]{1,0:T(8,128)S(1)} %broadcast_in_dim.33.lens, bf16[3584,128]{1,0:T(8,128)(2,1)S(1)} %pack_near.1.packed.near_packed, bf16[32,32,128]{2,1,0:T(8,128)(2,1)S(1)} %collective-permute-done.1.qa.q1a, ...), custom_call_target="tpu_custom_call" | custom-call | flops 1024 | bytes 1024 | tf_op jit(solution)/shard_map/early/pallas_call | solution.py:248
  32.1 0.0 collective-permute-done.4
  32.1 0.2 collective-permute-done.3
  32.3 0.1 add.72.qa.q2a
  32.4 1.4 %collective-permute-start.6 = (bf16[32,32,128]{2,1,0:T(8,128)(2,1)S(1)}, bf16[32,32,128]{2,1,0:T(8,128)(2,1)S(1)}, u32[]{:S(2)}, u32[]{:S(2)}) collective-permute-start(bf16[32,32,128]{2,1,0:T(8,128)(2,1)S(1)} %add.72.qa.q2a), channel_id=1, source_target_pairs={{0,1},{1,0},{2,3},{3,2},{4,5},{5,4},{6,7},{7,6},{8,9},{9,8},{10,11... | collective-permute-start | bytes 786440 | tf_op jit(solution)/shard_map/ppermute | solution.py:215
  33.8 0.0 collective-permute-done.7.far
  33.8 1.9 %middle.1 = (bf16[2048,128]{1,0:T(8,128)(2,1)S(1)}, f32[32,2048]{1,0:T(8,128)S(1)}) custom-call(s32[13]{0:T(128)S(1)} %select_reduce_fusion.2.starts, s32[32,128]{1,0:T(8,128)S(1)} %broadcast_in_dim.33.lens, bf16[128,128]{1,0:T(8,128)(2,1)S(1)} %and_convert_fusion.sort, s32[128,128]{1,0:T(8,128)S(1)} %broadcast_in_dim.35.tall, ...), custom_call_target="tpu_custom_call" | custom-call | flops 1024 | bytes 1024 | tf_op jit(solution)/shard_map/middle/pallas_call | solution.py:248
  35.7 0.0 collective-permute-done.6.qb.q2b
  35.7 4.6 %second.1.old2 = f32[32,2048]{1,0:T(8,128)S(1)} custom-call(s32[13]{0:T(128)S(1)} %select_reduce_fusion.2.starts, s32[32,128]{1,0:T(8,128)S(1)} %broadcast_in_dim.33.lens, bf16[3584,128]{1,0:T(8,128)(2,1)S(1)} %pack_near.1.packed.near_packed, bf16[2048,128]{1,0:T(8,128)(2,1)S(1)} %get-tuple-element.26.far_packed, bf16[32,32,128]{2,1,0:T(8,128)(2,1)S(1)} %add.72.qa.q2a, ...), custom_call_target="tpu_custom_call" | custom-call | flops 1024 | bytes 1024 | tf_op jit(solution)/shard_map/second/pallas_call | solution.py:248
  40.4 0.0 collective-permute-done.far
  40.4 2.6 %late.1 = f32[32,128]{1,0:T(8,128)S(1)} custom-call(s32[13]{0:T(128)S(1)} %select_reduce_fusion.2.starts, s32[32]{0:T(128)S(1)} %get-tuple-element.27.order, s32[32,128]{1,0:T(8,128)S(1)} %broadcast_in_dim.33.lens, bf16[128,128]{1,0:T(8,128)(2,1)S(1)} %and_convert_fusion.sort, s32[128,128]{1,0:T(8,128)S(1)} %broadcast_in_dim.35.tall, ...), custom_call_target="tpu_custom_call" | custom-call | flops 1024 | bytes 1024 | tf_op jit(solution)/shard_map/late/pallas_call | solution.py:248
  43.0 1.7 %collective-permute-start.8 = (f32[32,128]{1,0:T(8,128)S(1)}, f32[32,128]{1,0:T(8,128)S(1)}, u32[]{:S(2)}, u32[]{:S(2)}) collective-permute-start(f32[32,128]{1,0:T(8,128)S(1)} %late.1), channel_id=1, source_target_pairs={{0,1},{1,0},{2,3},{3,2},{4,5},{5,4},{6,7},{7,6},{8,9},{9,8},{10,11... | collective-permute-start | bytes 49160 | tf_op jit(solution)/shard_map/ppermute | solution.py:215
  44.6 0.8 %collective-permute-done.8 = f32[32,128]{1,0:T(8,128)S(1)} collective-permute-done((f32[32,128]{1,0:T(8,128)S(1)}, f32[32,128]{1,0:T(8,128)S(1)}, u32[]{:S(2)}, u32[]{:S(2)}) %collective-permute-start.8) | collective-permute-done | bytes 16416 | tf_op jit(solution)/shard_map/ppermute | solution.py:215
  45.5 0.1 slice_select_fusion
  45.6 3.1 %collective-permute-start.9 = (f32[64,64]{1,0:T(8,128)S(1)}, f32[64,64]{1,0:T(8,128)S(1)}, u32[]{:S(2)}, u32[]{:S(2)}) collective-permute-start(f32[64,64]{1,0:T(8,128)S(1)} %slice_select_fusion), channel_id=1, source_target_pairs={{0,4},{1,9},{2,6},{3,11},{4,8},{5,13},{6,10},{7,15},{8,12},{9,17},... | collective-permute-start | bytes 49160 | tf_op jit(solution)/shard_map/ppermute | solution.py:225
  48.7 0.3 collective-permute-start.10
  49.0 4.6 %collective-permute-done.9 = f32[64,64]{1,0:T(8,128)S(1)} collective-permute-done((f32[64,64]{1,0:T(8,128)S(1)}, f32[64,64]{1,0:T(8,128)S(1)}, u32[]{:S(2)}, u32[]{:S(2)}) %collective-permute-start.9) | collective-permute-done | bytes 16416 | tf_op jit(solution)/shard_map/ppermute | solution.py:225
  53.6 4.3 %collective-permute-done.10 = f32[64,64]{1,0:T(8,128)S(1)} collective-permute-done((f32[64,64]{1,0:T(8,128)S(1)}, f32[64,64]{1,0:T(8,128)S(1)}, u32[]{:S(2)}, u32[]{:S(2)}) %collective-permute-start.10) | collective-permute-done | bytes 16416 | tf_op jit(solution)/shard_map/ppermute | solution.py:225
  57.9 1.0 %collective-permute-start.11 = (f32[128,64]{1,0:T(8,128)S(1)}, f32[128,64]{1,0:T(8,128)S(1)}, u32[]{:S(2)}, u32[]{:S(2)}) collective-permute-start(f32[128,64]{1,0:T(8,128)S(1)} %maximum_select_fusion.2), channel_id=1, source_target_pairs={{0,1},{1,0},{2,3},{3,2},{4,5},{5,4},{6,7},{7,6},{8,9},{9,8},{10,11... | collective-permute-start | bytes 98312 | tf_op jit(solution)/shard_map/ppermute | solution.py:215
  58.8 0.9 %collective-permute-done.11 = f32[128,64]{1,0:T(8,128)S(1)} collective-permute-done((f32[128,64]{1,0:T(8,128)S(1)}, f32[128,64]{1,0:T(8,128)S(1)}, u32[]{:S(2)}, u32[]{:S(2)}) %collective-permute-start.11) | collective-permute-done | bytes 32800 | tf_op jit(solution)/shard_map/ppermute | solution.py:215
  59.7 0.7 %copy.6 = f32[64,2,128]{2,1,0:T(2,128)} copy(f32[64,2,128]{0,2,1:T(8,128)S(1)} %fusion) | data formatting | bytes 131072 | tf_op jit(solution)/shard_map/transpose | solution.py:342
  (11 shorter events, 0.1 us)
Async XLA Ops:
  0.0 1.0 %copy-start = (bf16[64,32,128]{2,1,0:T(8,128)(2,1)S(1)}, bf16[64,32,128]{2,1,0:T(8,128)(2,1)}, u32[]{:S(2)}) copy-start(bf16[64,32,128]{2,1,0:T(8,128)(2,1)} %param.4) | copy-start | bytes 1572868
  1.1 21.6 %copy-start.2 = (s32[4]{0:T(128)S(1)}, s32[4]{0:T(128)}, u32[]{:S(2)}) copy-start(s32[4]{0:T(128)} %constant.75.clone) | copy-start | bytes 52
  1.7 11.1 %copy-start.1 = (bf16[32,32,128]{2,1,0:T(8,128)(2,1)}, bf16[32,32,128]{2,1,0:T(8,128)(2,1)S(1)}, u32[]{:S(2)}) copy-start(bf16[32,32,128]{2,1,0:T(8,128)(2,1)S(1)} %prepare.1.after_ref) | copy-start | bytes 786436
  1.7 21.3 %collective-permute-start.1 = (bf16[32,32,128]{2,1,0:T(8,128)(2,1)S(1)}, bf16[32,32,128]{2,1,0:T(8,128)(2,1)S(1)}, u32[]{:S(2)}, u32[]{:S(2)}) collective-permute-start(bf16[32,32,128]{2,1,0:T(8,128)(2,1)S(1)} %prepare.1.after_ref), channel_id=1, source_target_pairs={{0,252},{1,255},{2,254},{3,253},{4,0},{5,1},{6,2},{7,3},{8,4},{9,5... | collective-permute-start | bytes 786440 | tf_op jit(solution)/shard_map/ppermute | solution.py:211
  15.1 9.7 %collective-permute-start.5 = (bf16[45,32,128]{2,1,0:T(8,128)(2,1)}, bf16[45,32,128]{2,1,0:T(8,128)(2,1)S(1)}, u32[]{:S(2)}, u32[]{:S(2)}) collective-permute-start(bf16[45,32,128]{2,1,0:T(8,128)(2,1)} %get-tuple-element.21), channel_id=1, source_target_pairs={{0,1},{1,0},{2,3},{3,2},{4,5},{5,4},{6,7},{7,6},{8,9},{9,8},{10,11... | collective-permute-start | bytes 1105928 | tf_op jit(solution)/shard_map/ppermute | solution.py:215
  15.2 16.9 %collective-permute-start.4 = (bf16[32,32,128]{2,1,0:T(8,128)(2,1)}, bf16[32,32,128]{2,1,0:T(8,128)(2,1)S(1)}, u32[]{:S(2)}, u32[]{:S(2)}) collective-permute-start(bf16[32,32,128]{2,1,0:T(8,128)(2,1)} %copy-done.1), channel_id=1, source_target_pairs={{0,248},{1,251},{2,250},{3,249},{4,252},{5,255},{6,254},{7,253},{3... | collective-permute-start | bytes 786440 | tf_op jit(solution)/shard_map/ppermute | solution.py:211
  19.2 14.6 %collective-permute-start.7 = (bf16[45,32,128]{2,1,0:T(8,128)(2,1)}, bf16[45,32,128]{2,1,0:T(8,128)(2,1)S(1)}, u32[]{:S(2)}, u32[]{:S(2)}) collective-permute-start(bf16[45,32,128]{2,1,0:T(8,128)(2,1)} %get-tuple-element.23), channel_id=1, source_target_pairs={{0,3},{1,2},{2,1},{3,0},{4,7},{5,6},{6,5},{7,4},{8,11},{9,10},{10,... | collective-permute-start | bytes 1105928 | tf_op jit(solution)/shard_map/ppermute | solution.py:215
  23.0 5.4 %collective-permute-start.2 = (bf16[32,32,128]{2,1,0:T(8,128)(2,1)S(1)}, bf16[32,32,128]{2,1,0:T(8,128)(2,1)S(1)}, u32[]{:S(2)}, u32[]{:S(2)}) collective-permute-start(bf16[32,32,128]{2,1,0:T(8,128)(2,1)S(1)} %collective-permute-done.1.qa.q1a), channel_id=1, source_target_pairs={{0,1},{1,0},{2,3},{3,2},{4,5},{5,4},{6,7},{7,6},{8,9},{9,8},{10,11... | collective-permute-start | bytes 786440 | tf_op jit(solution)/shard_map/ppermute | solution.py:215
  23.0 9.3 %collective-permute-start.3 = (bf16[32,32,128]{2,1,0:T(8,128)(2,1)S(1)}, bf16[32,32,128]{2,1,0:T(8,128)(2,1)S(1)}, u32[]{:S(2)}, u32[]{:S(2)}) collective-permute-start(bf16[32,32,128]{2,1,0:T(8,128)(2,1)S(1)} %collective-permute-done.1.qa.q1a), channel_id=1, source_target_pairs={{4,0},{5,1},{6,2},{7,3},{8,4},{9,5},{10,6},{11,7},{12,8},{13,9},{1... | collective-permute-start | bytes 786440 | tf_op jit(solution)/shard_map/ppermute | solution.py:211
  24.8 15.6 %collective-permute-start = (bf16[45,32,128]{2,1,0:T(8,128)(2,1)}, bf16[45,32,128]{2,1,0:T(8,128)(2,1)S(1)}, u32[]{:S(2)}, u32[]{:S(2)}) collective-permute-start(bf16[45,32,128]{2,1,0:T(8,128)(2,1)} %get-tuple-element.17), channel_id=1, source_target_pairs={{0,2},{1,3},{2,0},{3,1},{4,6},{5,7},{6,4},{7,5},{8,10},{9,11},{10,... | collective-permute-start | bytes 1105928 | tf_op jit(solution)/shard_map/ppermute | solution.py:215
  32.4 3.3 %collective-permute-start.6 = (bf16[32,32,128]{2,1,0:T(8,128)(2,1)S(1)}, bf16[32,32,128]{2,1,0:T(8,128)(2,1)S(1)}, u32[]{:S(2)}, u32[]{:S(2)}) collective-permute-start(bf16[32,32,128]{2,1,0:T(8,128)(2,1)S(1)} %add.72.qa.q2a), channel_id=1, source_target_pairs={{0,1},{1,0},{2,3},{3,2},{4,5},{5,4},{6,7},{7,6},{8,9},{9,8},{10,11... | collective-permute-start | bytes 786440 | tf_op jit(solution)/shard_map/ppermute | solution.py:215
  43.0 2.5 %collective-permute-start.8 = (f32[32,128]{1,0:T(8,128)S(1)}, f32[32,128]{1,0:T(8,128)S(1)}, u32[]{:S(2)}, u32[]{:S(2)}) collective-permute-start(f32[32,128]{1,0:T(8,128)S(1)} %late.1), channel_id=1, source_target_pairs={{0,1},{1,0},{2,3},{3,2},{4,5},{5,4},{6,7},{7,6},{8,9},{9,8},{10,11... | collective-permute-start | bytes 49160 | tf_op jit(solution)/shard_map/ppermute | solution.py:215
  45.6 8.0 %collective-permute-start.9 = (f32[64,64]{1,0:T(8,128)S(1)}, f32[64,64]{1,0:T(8,128)S(1)}, u32[]{:S(2)}, u32[]{:S(2)}) collective-permute-start(f32[64,64]{1,0:T(8,128)S(1)} %slice_select_fusion), channel_id=1, source_target_pairs={{0,4},{1,9},{2,6},{3,11},{4,8},{5,13},{6,10},{7,15},{8,12},{9,17},... | collective-permute-start | bytes 49160 | tf_op jit(solution)/shard_map/ppermute | solution.py:225
  48.7 9.2 %collective-permute-start.10 = (f32[64,64]{1,0:T(8,128)S(1)}, f32[64,64]{1,0:T(8,128)S(1)}, u32[]{:S(2)}, u32[]{:S(2)}) collective-permute-start(f32[64,64]{1,0:T(8,128)S(1)} %slice_select_fusion), channel_id=1, source_target_pairs={{0,6},{1,11},{2,4},{3,9},{4,10},{5,15},{6,8},{7,13},{8,14},{9,19},... | collective-permute-start | bytes 49160 | tf_op jit(solution)/shard_map/ppermute | solution.py:225
  57.9 1.9 %collective-permute-start.11 = (f32[128,64]{1,0:T(8,128)S(1)}, f32[128,64]{1,0:T(8,128)S(1)}, u32[]{:S(2)}, u32[]{:S(2)}) collective-permute-start(f32[128,64]{1,0:T(8,128)S(1)} %maximum_select_fusion.2), channel_id=1, source_target_pairs={{0,1},{1,0},{2,3},{3,2},{4,5},{5,4},{6,7},{7,6},{8,9},{9,8},{10,11... | collective-permute-start | bytes 98312 | tf_op jit(solution)/shard_map/ppermute | solution.py:215
